TPU v7x, 512 devices: a whole 4x4x16 slice. The times are simulated.
512 devices in a mesh: res: 32 (over z, x_lo), seq: 16 (over y, x_hi, core).
Axes of the slice: x: 4 (x_hi: 2, x_lo: 2; x = x_hi * 2 + x_lo), y: 4, z: 16, core: 2. Of those that a mesh axis runs over, the one named last changes fastest.
Arguments:
- alignment_input: bfloat16 [256, 1024, 256], P('seq', 'res'), may hold values from -8 to 8
- alignment_mask: int32 [256, 1024], P('seq', 'res'), may hold values from 0 to 1, as said below
- residue_present_mask: int32 [1024], P('res'), may hold values 0 or 1
- layer_norm_gain: float32 [256], replicated, may hold values from 0.1 to 1.9
- layer_norm_bias: float32 [256], replicated, may hold values from -3 to 3
- projection_weight: bfloat16 [256, 64], replicated, may hold values from -0.375 to 0.375
- projection_bias: float32 [64], replicated, may hold values from -4 to 4
- output_weight: bfloat16 [1024, 128], replicated, may hold values from -0.1875 to 0.1875
- output_bias: float32 [128], replicated, may hold values from -3 to 3
Outputs:
- pair_update: float32 [1024, 1024, 128], P('res', 'seq')
Inputs may be any that keep to these rules, and one draw needn't show every extreme that they name: `alignment_mask`: 1 marks a present MSA entry.
All inputs are finite; a program needn't handle non-finite values. No bound on the sum of `residue_present_mask` on one device may be relied on, other than what follows from the above.
Results may differ from a plain program's by a relative error of at most 0.003.
Values may be sent and summed in bfloat16 or wider, within the bound.
No kernel may reach another device: no remote copies, remote signals or barrier semaphores. Data moves between devices by JAX's collectives and lax.ppermute only.
A program may use at most 64 MiB of HBM per device.

v0:
```python
import jax
import jax.numpy as jnp
from jax import lax
from jax.sharding import PartitionSpec as P

EPSILON = 1e-05


def spread(block, axis, holder):
    block = jnp.where(lax.axis_index(axis) == holder, block, jnp.zeros_like(block))
    return lax.psum(block, axis)


def project_alignment(
    alignment_input,
    alignment_mask,
    residue_present_mask,
    layer_norm_gain,
    layer_norm_bias,
    projection_weight,
    projection_bias,
):
    weight_array = (alignment_mask * residue_present_mask[None, :]).astype(jnp.float32)
    value_array = alignment_input.astype(jnp.float32)
    channel_mean = jnp.mean(value_array, axis=-1, keepdims=True)
    centred = value_array - channel_mean
    channel_var = jnp.mean(centred * centred, axis=-1, keepdims=True)
    normalized_input = (
        centred * lax.rsqrt(channel_var + EPSILON) * layer_norm_gain + layer_norm_bias
    ).astype(jnp.bfloat16)
    sequence_total, residue_total, alignment_channels = alignment_input.shape
    projected_sides = jnp.dot(
        normalized_input.reshape(sequence_total * residue_total, alignment_channels),
        projection_weight,
        preferred_element_type=jnp.float32,
    )
    projected_sides = projected_sides.reshape(sequence_total, residue_total, -1) + projection_bias
    projected_sides = (projected_sides * weight_array[:, :, None]).astype(jnp.bfloat16)
    return (projected_sides, weight_array)


def pair_tile(row_act, row_weights, col_act, col_weights, output_weight, output_bias, channels):
    row_count = row_weights.shape[1]
    col_count = col_weights.shape[1]
    outer_sum = lax.dot_general(
        row_act, col_act, (((0,), (0,)), ((), ())), preferred_element_type=jnp.float32
    )
    outer_sum = outer_sum.reshape(row_count, channels, col_count, channels).transpose(0, 2, 1, 3)
    outer_sum = outer_sum.reshape(row_count * col_count, channels * channels).astype(jnp.bfloat16)
    update = jnp.dot(outer_sum, output_weight, preferred_element_type=jnp.float32)
    update = update.reshape(row_count, col_count, -1) + output_bias
    pair_count = lax.dot_general(
        row_weights, col_weights, (((0,), (0,)), ((), ())), preferred_element_type=jnp.float32
    )
    return update / jnp.maximum(pair_count, 1.0)[:, :, None]


def local(
    alignment_input,
    alignment_mask,
    residue_present_mask,
    layer_norm_gain,
    layer_norm_bias,
    projection_weight,
    projection_bias,
    output_weight,
    output_bias,
):
    projected_sides, weight_array = project_alignment(
        alignment_input,
        alignment_mask,
        residue_present_mask,
        layer_norm_gain,
        layer_norm_bias,
        projection_weight,
        projection_bias,
    )
    sequence_total, residue_total, proj_width = projected_sides.shape
    channels = proj_width // 2
    row_act = projected_sides[:, :, :channels].reshape(sequence_total, residue_total * channels)
    col_act = projected_sides[:, :, channels:].reshape(sequence_total, residue_total * channels)
    local_weights = weight_array.astype(jnp.bfloat16)
    block_ratio = lax.axis_size("res") // lax.axis_size("seq")
    column_tiles = []
    rows_all, cols_all, weights_all = (
        lax.all_gather(row_act, "seq", axis=0, tiled=True),
        lax.all_gather(col_act, "seq", axis=0, tiled=True),
        lax.all_gather(local_weights, "seq", axis=0, tiled=True),
    )
    first_block = lax.axis_index("seq") * block_ratio
    for segment in range(block_ratio):
        block_act, block_weights = (
            spread(cols_all, "res", first_block + segment),
            spread(weights_all, "res", first_block + segment),
        )
        column_tiles.append(
            pair_tile(
                rows_all,
                weights_all,
                block_act,
                block_weights,
                output_weight,
                output_bias,
                channels,
            )
        )
    return jnp.concatenate(column_tiles, axis=1)


def solution(mesh):
    in_specs = (P("seq", "res", None), P("seq", "res"), P("res"), P(), P(), P(), P(), P(), P())
    out_specs = P("res", "seq", None)
    return jax.shard_map(local, mesh=mesh, in_specs=in_specs, out_specs=out_specs, check_vma=False)
```

profile of v0, /device:TPU:8, one launch (start us, length us, event | category | flops | bytes accessed | tf_op | source)
XLA Modules:
  0.0 379.6 jit_solution(1134897722074380005)
XLA Ops:
  6.5 0.0 copy-start
  6.5 0.0 all-reduce.4.cloned.1.call-start
  6.5 1.1 convert_reduce_fusion
  7.7 1.2 fusion.6
  8.9 0.7 fusion.18
  9.6 1.3 fusion.3
  10.9 0.1 fusion.19
  11.1 0.2 reshape.45
  11.2 24.7 %all_gather.10 = bf16[256,1024]{1,0:T(8,128)(2,1)S(1)} all-gather(bf16[16,1024]{1,0:T(8,128)(2,1)S(1)} %reshape.45), channel_id=1, replica_groups=mesh['res'=32,'seq'=16] {'seq'}, dimensions={0}, use_global_device_ids=true | all-gather | bytes 557056 | tf_op jit(solution)/shard_map/all_gather | solution.py:87
  35.9 1.0 broadcast_select_fusion.1
  36.9 0.0 all-reduce.4.cloned.1.call-update
  36.9 0.2 reshape.44
  37.1 22.4 %all_gather.11 = bf16[256,32]{1,0:T(8,128)(2,1)S(1)} all-gather(bf16[16,32]{1,0:T(8,128)(2,1)S(1)} %get-tuple-element.9), channel_id=1, replica_groups=mesh['res'=32,'seq'=16] {'seq'}, dimensions={0}, use_global_device_ids=true | all-gather | bytes 17408 | tf_op jit(solution)/shard_map/all_gather | solution.py:88
  59.5 125.0 %all-reduce = (bf16[256,32]{1,0:T(8,128)(2,1)S(1)}, bf16[256,32]{1,0:T(8,128)(2,1)S(1)}) all-reduce(bf16[256,32]{1,0:T(8,128)(2,1)S(1)} %get-tuple-element.16, bf16[256,32]{1,0:T(8,128)(2,1)S(1)} %get-tuple-element.15), channel_id=1, replica_groups=mesh['res'=32,'seq'=16] {'res'}, use_global_device_ids=true, to_apply=%region_5.6 | all-reduce | flops 16384 | bytes 65536 | tf_op jit(solution)/shard_map/psum | solution.py:11
  184.6 0.2 convolution_maximum_fusion.1
  184.7 0.2 convolution_maximum_fusion
  184.9 25.4 %all_gather.9 = bf16[256,1024]{1,0:T(8,128)(2,1)S(1)} all-gather(bf16[16,1024]{1,0:T(8,128)(2,1)S(1)} %reshape.44), channel_id=1, replica_groups=mesh['res'=32,'seq'=16] {'seq'}, dimensions={0}, use_global_device_ids=true | all-gather | bytes 557056 | tf_op jit(solution)/shard_map/all_gather | solution.py:86
  210.3 94.6 %all-reduce.4.cloned.1.call-done = (bf16[256,1024]{1,0:T(8,128)(2,1)}, bf16[256,1024]{1,0:T(8,128)(2,1)}) async-done(((bf16[256,1024]{1,0:T(8,128)(2,1)}, bf16[256,1024]{1,0:T(8,128)(2,1)}), (bf16[256,1024]{1,0:T(8,128)(2,1)}, bf16[256,1024]{1,0:T(8,128)(2,1)})) %all-reduce.4.cloned.1.call-update) | async-done | bytes 1048592 | tf_op jit(solution)/shard_map/psum | solution.py:11
  304.9 1.8 convolution_convert_fusion.1
  306.7 8.0 %convert_element_type.46 = bf16[32,32,32,32]{3,2,1,0:T(8,128)(2,1)} reshape(bf16[1024,1024]{1,0:T(8,128)(2,1)S(1)} %convolution_convert_fusion.1) | data formatting | bytes 4194304 | tf_op jit(solution)/shard_map/convert_element_type | solution.py:49
  314.6 10.5 %copy.10 = bf16[32,32,32,32]{3,2,1,0:T(8,128)(2,1)} copy(bf16[32,32,32,32]{3,1,2,0:T(8,128)(2,1)} %bitcast.24) | data formatting | bytes 4194304 | tf_op jit(solution)/shard_map/convert_element_type | solution.py:49
  325.2 0.0 copy-start.3
  325.2 12.4 %convert_element_type.48 = bf16[32,32,1024]{2,1,0:T(8,128)(2,1)} reshape(bf16[32,32,32,32]{3,2,1,0:T(8,128)(2,1)} %copy.10) | data formatting | bytes 4194304 | tf_op jit(solution)/shard_map/convert_element_type | solution.py:49
  337.6 0.0 copy-done.3
  337.6 0.7 convolution_convert_fusion
  338.4 8.0 %convert_element_type.51 = bf16[32,32,32,32]{3,2,1,0:T(8,128)(2,1)} reshape(bf16[1024,1024]{1,0:T(8,128)(2,1)S(1)} %convolution_convert_fusion) | data formatting | bytes 4194304 | tf_op jit(solution)/shard_map/convert_element_type | solution.py:49
  346.3 10.5 %copy.11 = bf16[32,32,32,32]{3,2,1,0:T(8,128)(2,1)} copy(bf16[32,32,32,32]{3,1,2,0:T(8,128)(2,1)} %bitcast.25) | data formatting | bytes 4194304 | tf_op jit(solution)/shard_map/convert_element_type | solution.py:49
  356.8 0.0 copy-start.1
  356.8 0.0 copy-start.4
  356.8 12.5 %convert_element_type.53 = bf16[32,32,1024]{2,1,0:T(8,128)(2,1)} reshape(bf16[32,32,32,32]{3,2,1,0:T(8,128)(2,1)} %copy.11) | data formatting | bytes 4194304 | tf_op jit(solution)/shard_map/convert_element_type | solution.py:49
  369.4 0.0 copy-done
  369.4 0.0 copy-done.1
  369.4 0.0 copy-done.4
  369.4 0.0 copy-start.2
  369.4 0.7 fusion.1
  370.1 0.9 copy-done.2
  371.0 0.7 fusion
  371.7 1.1 pad_maximum_fusion
  (3 shorter events, 0.0 us)
Async XLA Ops:
  6.5 362.8 %copy-start = (bf16[1024,128]{1,0:T(8,128)(2,1)S(1)}, bf16[1024,128]{1,0:T(8,128)(2,1)}, u32[]{:S(2)}) copy-start(bf16[1024,128]{1,0:T(8,128)(2,1)} %param.16) | copy-start | bytes 786436
  6.5 298.4 %all-reduce.4.cloned.1.call-start = ((), (), s32[]{:S(2)}) async-start(), calls=%async_computation | async-start | bytes 2097152 | tf_op jit(solution)/shard_map/psum | solution.py:11
  325.2 12.4 %copy-start.3 = (bf16[256,1024]{1,0:T(8,128)(2,1)S(1)}, bf16[256,1024]{1,0:T(8,128)(2,1)}, u32[]{:S(2)}) copy-start(bf16[256,1024]{1,0:T(8,128)(2,1)} %get-tuple-element.7) | copy-start | bytes 1572868
  356.8 12.5 %copy-start.1 = (bf16[32,32,1024]{2,1,0:T(8,128)(2,1)S(1)}, bf16[32,32,1024]{2,1,0:T(8,128)(2,1)}, u32[]{:S(2)}) copy-start(bf16[32,32,1024]{2,1,0:T(8,128)(2,1)} %convert_element_type.48) | copy-start | bytes 6291460
  356.8 12.5 %copy-start.4 = (f32[128]{0:T(128)S(1)}, f32[128]{0:T(128)}, u32[]{:S(2)}) copy-start(f32[128]{0:T(128)} %param.17) | copy-start | bytes 1540
  369.4 1.6 copy-start.2
Sparse Core Ops, SparseCore 0:
  37.1 267.7 all-reduce.3
where the time goes:
time: 380 us
  blocking collectives  197 us (52%)
  waiting for transfers between devices  94.6 us (25%)
  local copies, waits for them, and re-layouts  63.3 us (17%)
  between operations  13.5 us (4%)
  matrix products  5.61 us (1%)
  other arithmetic  5.16 us (1%)
    psum x1, blocking collectives, spread(): return lax.psum(block, axis)  125 us
    psum x1, waiting for transfers between devices, spread(): return lax.psum(block, axis)  94.6 us
    convert_element_type x6, local copies, waits for them, and re-layouts, pair_tile(): outer_sum.reshape(row_count * col_count, channels * channels)  61.9 us
    all_gather x1, blocking collectives, local(): lax.all_gather(row_act, 'seq', axis=0, tiled=True)  25.4 us
    all_gather x1, blocking collectives, local(): lax.all_gather(col_act, 'seq', axis=0, tiled=True)  24.7 us
    all_gather x1, blocking collectives, local(): lax.all_gather(local_weights, 'seq', axis=0, tiled=True)  22.4 us
  transfers between devices with their start and end apart: 1, of which 1 were waited for; matrix products, arithmetic and copies ran while one was open for 0% of the time, Pallas kernels for 0%

commit v1 on v0

v1 whole, which is shorter than its diff:
```python
import jax
import jax.numpy as jnp
from jax import lax
from jax.experimental import pallas as pl
from jax.experimental.pallas import tpu as pltpu
from jax.sharding import Mesh, PartitionSpec as P

EPSILON = 1e-05
SEQ = ("y", "xh", "core")
RES = ("z", "xl")


def project(x, mask, present, gain, bias, weight, proj_bias):
    weights = (mask * present[None, :]).astype(jnp.float32)
    value = x.astype(jnp.float32)
    mean = jnp.mean(value, axis=-1, keepdims=True)
    centred = value - mean
    var = jnp.mean(centred * centred, axis=-1, keepdims=True)
    normed = (centred * lax.rsqrt(var + EPSILON) * gain + bias).astype(jnp.bfloat16)
    s, r, w = x.shape
    proj = jnp.dot(normed.reshape(s * r, w), weight, preferred_element_type=jnp.float32)
    proj = proj.reshape(s, r, -1) + proj_bias
    return (proj * weights[:, :, None]).astype(jnp.bfloat16), weights.astype(jnp.bfloat16)


def pair_kernel(at_ref, b_ref, w_ref, bias_ref, o_ref, bint, xs):
    lane = lax.broadcasted_iota(jnp.int32, (256, 128), 1)
    odd = (lane // 32) % 2 == 1
    for g in range(8):
        v0 = b_ref[0, :, g * 128:(g + 1) * 128].astype(jnp.float32)
        v1 = b_ref[1, :, g * 128:(g + 1) * 128].astype(jnp.float32)
        bint[:, (2 * g) * 128:(2 * g + 1) * 128] = jnp.where(odd, pltpu.roll(v1, 32, 1), v0).astype(jnp.bfloat16)
        bint[:, (2 * g + 1) * 128:(2 * g + 2) * 128] = jnp.where(odd, v1, pltpu.roll(v0, 96, 1)).astype(jnp.bfloat16)
    w0 = b_ref[0, :, 1024:1152].astype(jnp.float32)
    w1 = b_ref[1, :, 1024:1152].astype(jnp.float32)
    wb = w0 + pltpu.roll(w1, 32, 1)
    wb = (wb + pltpu.roll(wb, 64, 1)).astype(jnp.bfloat16)
    count = jnp.dot(at_ref[1024:1056, :], wb, preferred_element_type=jnp.float32)
    low = lax.broadcasted_iota(jnp.int32, (16, 128), 1) < 64
    inv = 1.0 / jnp.maximum(jnp.where(low, count[:16], count[16:]), 1.0)
    bias = bias_ref[...]
    low = lax.broadcasted_iota(jnp.int32, (128, 128), 1) < 64
    for n in range(8):
        for m in range(4):
            o = jnp.dot(at_ref[m * 256:(m + 1) * 256, :], bint[:, n * 256:(n + 1) * 256],
                        preferred_element_type=jnp.float32).astype(jnp.bfloat16)
            for k in range(8):
                i = m * 8 + k
                for t in range(2):
                    h = 2 * n + t
                    xs[i // 2, h * 32:(h + 1) * 32, (i % 2) * 128:(i % 2 + 1) * 128] = (
                        o[k * 32:(k + 1) * 32, t * 128:(t + 1) * 128])
    for ip in range(16):
        y = jnp.dot(w_ref[...], xs[ip], preferred_element_type=jnp.float32)
        t0, b0, t1, b1 = y[:128, :128], y[128:, :128], y[:128, 128:], y[128:, 128:]
        u = jnp.where(low, t0, b1)
        v = jnp.where(low, t1, b0)
        z = (u + pltpu.roll(v, 64, 1) + bias) * inv[ip:ip + 1]
        zt = z.T
        o_ref[2 * ip] = zt[:64]
        o_ref[2 * ip + 1] = zt[64:]


def pair(at, b, w2, bias):
    return pl.pallas_call(
        pair_kernel,
        out_shape=jax.ShapeDtypeStruct((32, 64, 128), jnp.float32),
        in_specs=[pl.BlockSpec(memory_space=pltpu.VMEM)] * 4,
        out_specs=pl.BlockSpec(memory_space=pltpu.VMEM),
        scratch_shapes=[pltpu.VMEM((256, 2048), jnp.bfloat16), pltpu.VMEM((16, 512, 256), jnp.bfloat16)],
        compiler_params=pltpu.CompilerParams(vmem_limit_bytes=40 * 1024 * 1024),
        cost_estimate=pl.CostEstimate(flops=2 * 10**9, bytes_accessed=4 * 2**20, transcendentals=0),
        name="pair",
    )(at, b, w2, bias)


def local(x, mask, present, gain, bias, weight, proj_bias, out_weight, out_bias):
    proj, weights = project(x, mask, present, gain, bias, weight, proj_bias)
    s, r, _ = proj.shape
    zeros = jnp.zeros((s, 96), jnp.bfloat16)
    even_odd = weights.reshape(s, r // 2, 2).transpose(0, 2, 1).reshape(s, r)
    a = jnp.concatenate([proj[:, :, :32].reshape(s, r * 32), even_odd, zeros], axis=1)
    bt = proj[:, :, 32:].transpose(0, 2, 1).reshape(s, 8, 2, 2, r).transpose(0, 1, 3, 2, 4)
    b = jnp.concatenate([bt.reshape(s, r * 32), weights, zeros], axis=1)
    a_all = lax.all_to_all(jnp.broadcast_to(a[None], (16, *a.shape)), SEQ, 0, 0, tiled=True)
    b_z = lax.all_to_all(jnp.broadcast_to(b[None], (16, *b.shape)), "z", 0, 0, tiled=True)
    b_two = jnp.concatenate([b_z, b_z], axis=0)
    b_all = lax.all_to_all(b_two, ("xl",) + SEQ, 0, 0, tiled=True).reshape(2, 256, 1152)
    at = a_all.reshape(256, 1152).T
    w2 = out_weight.reshape(32, 16, 2, 128).transpose(2, 3, 1, 0).reshape(256, 512)
    bias2 = jnp.broadcast_to(out_bias[:, None], (128, 128))
    return pair(at, b_all, w2, bias2)


def solution(mesh):
    fine = Mesh(mesh.devices.reshape(16, 2, 4, 2, 2), ("z", "xl", "y", "xh", "core"))
    in_specs = (P(SEQ, RES, None), P(SEQ, RES), P(RES), P(), P(), P(), P(), P(), P())
    return jax.shard_map(local, mesh=fine, in_specs=in_specs, out_specs=P(RES, SEQ, None), check_vma=False)
```

time: 380 us -> 101 us (0.27)
  the two profiles are of different devices: /device:TPU:8 before, /device:TPU:1 now
where the time goes in v1:
time: 101 us; the launch traced here: 100 us
  waiting for transfers between devices  53.5 us (53%)
  starting transfers between devices  33.9 us (34%)
  other arithmetic  4.15 us (4%)
  Pallas kernels  3.76 us (4%)
  local copies, waits for them, and re-layouts  3.65 us (4%)
  matrix products  1.3 us (1%)
    all_to_all x1, waiting for transfers between devices, local(): lax.all_to_all(jnp.broadcast_to(b[None], (16, *b.shape)), 'z', 0, 0, tile...  24.8 us
    all_to_all x1, waiting for transfers between devices, local(): lax.all_to_all(b_two, ('xl',) + SEQ, 0, 0, tiled=True).reshape(2, 256, 1152)  17.9 us
    all_to_all x1, starting transfers between devices, local(): lax.all_to_all(jnp.broadcast_to(b[None], (16, *b.shape)), 'z', 0, 0, tile...  15.7 us
    all_to_all x1, starting transfers between devices, local(): lax.all_to_all(jnp.broadcast_to(a[None], (16, *a.shape)), SEQ, 0, 0, tile...  13.4 us
    all_to_all x1, waiting for transfers between devices, local(): lax.all_to_all(jnp.broadcast_to(a[None], (16, *a.shape)), SEQ, 0, 0, tile...  10.9 us
    all_to_all x1, starting transfers between devices, local(): lax.all_to_all(b_two, ('xl',) + SEQ, 0, 0, tiled=True).reshape(2, 256, 1152)  4.76 us
    pallas_call x1, Pallas kernels, pair(): pl.pallas_call(pair_kernel, out_shape=jax.ShapeDtypeStruct((32, 64, 128),...  3.76 us
  transfers between devices with their start and end apart: 3, of which 3 were waited for; matrix products, arithmetic and copies ran while one was open for 2% of the time, Pallas kernels for 0%

profile of v1, /device:TPU:1, one launch (start us, length us, event | category | flops | bytes accessed | tf_op | source)
XLA Modules:
  0.0 100.4 jit_solution(10378837026535766867)
XLA Ops:
  0.0 0.0 copy-start
  0.0 1.1 %convert_reduce_fusion = f32[16,32]{1,0:T(8,128)S(1)} fusion(bf16[16,32,256]{2,1,0:T(8,128)(2,1)} %param.9), kind=kLoop, calls=%fused_computation.5 | loop fusion | flops 261632 | bytes 264192 | tf_op jit(solution)/shard_map/reduce_sum | solution.py:16
  1.1 1.2 %fusion.4 = f32[16,32]{1,0:T(8,128)S(1)} fusion(bf16[16,32,256]{2,1,0:T(8,128)(2,1)} %param.9, f32[16,32]{1,0:T(8,128)S(1)} %broadcast_multiply_fusion), kind=kLoop, calls=%fused_computation.8 | loop fusion | flops 523776 | bytes 266240 | tf_op jit(solution)/shard_map/reduce_sum | solution.py:18
  2.3 0.7 fusion.14
  3.1 0.0 copy-done
  3.1 1.3 %fusion.1 = bf16[16,32,64]{2,1,0:T(8,128)(2,1)S(1)} fusion(bf16[16,32,256]{2,1,0:T(8,128)(2,1)} %param.9, f32[256]{0:T(256)} %param.13, f32[256]{0:T(256)} %param.12, f32[16,32]{1,0:T(8,128)S(1)} %add_rsqrt_fusion, f32[16,32]{1,0:T(8,128)S(1)} %broadcast_multiply_fusion, f32[16,32]{1,0:T(8,128)S(1)} %get-tuple-element.6, f32[64]{0:T(128)} %param.15, ...), kind=kOutput, calls=%fused_computation.3 | convolution fusion | flops 17661952 | bytes 368896 | tf_op jit(solution)/shard_map/dot_general | solution.py:21
  4.4 0.1 slice_bitcast_fusion
  4.5 0.2 copy.33
  4.7 0.1 copy.34
  4.8 0.2 reshape.56
  4.9 0.1 concatenate.10
  5.0 0.9 broadcast_in_dim.10
  5.9 15.7 %all-to-all-start.1 = ((bf16[16,16,1152]{2,1,0:T(8,128)(2,1)}), bf16[16,16,1152]{2,1,0:T(8,128)(2,1)S(1)}, u32[]{:S(2)}, u32[]{:S(2)}) async-start(bf16[16,16,1152]{2,1,0:T(8,128)(2,1)} %broadcast_in_dim.10), calls=%async_computation.1 | async-start | bytes 1179648 | tf_op jit(solution)/shard_map/all_to_all | solution.py:86
  21.6 0.1 copy.30
  21.7 0.2 reshape.51
  21.9 0.1 copy.31
  22.0 0.1 reshape.53
  22.1 0.1 concatenate.9
  22.2 24.8 %all-to-all-done.1 = bf16[16,16,1152]{2,1,0:T(8,128)(2,1)S(1)} async-done(((bf16[16,16,1152]{2,1,0:T(8,128)(2,1)}), bf16[16,16,1152]{2,1,0:T(8,128)(2,1)S(1)}, u32[]{:S(2)}, u32[]{:S(2)}) %all-to-all-start.1) | async-done | bytes 589856 | tf_op jit(solution)/shard_map/all_to_all | solution.py:86
  47.0 0.9 broadcast_in_dim.9
  47.8 13.4 %all-to-all-start = ((bf16[16,16,1152]{2,1,0:T(8,128)(2,1)}), bf16[16,16,1152]{2,1,0:T(8,128)(2,1)S(1)}, u32[]{:S(2)}, u32[]{:S(2)}) async-start(bf16[16,16,1152]{2,1,0:T(8,128)(2,1)} %broadcast_in_dim.9), calls=%async_computation | async-start | bytes 1179648 | tf_op jit(solution)/shard_map/all_to_all | solution.py:85
  61.2 1.1 %pad_maximum_fusion = bf16[32,16,1152]{2,1,0:T(8,128)(2,1)} fusion(bf16[16,16,1152]{2,1,0:T(8,128)(2,1)S(1)} %all-to-all-done.1), kind=kLoop, calls=%fused_computation | loop fusion | flops 589824 | bytes 1769472 | tf_op jit(solution)/shard_map/concatenate | solution.py:87
  62.4 0.0 copy-start.1
  62.4 10.9 %all-to-all-done = bf16[16,16,1152]{2,1,0:T(8,128)(2,1)S(1)} async-done(((bf16[16,16,1152]{2,1,0:T(8,128)(2,1)}), bf16[16,16,1152]{2,1,0:T(8,128)(2,1)S(1)}, u32[]{:S(2)}, u32[]{:S(2)}) %all-to-all-start) | async-done | bytes 589856 | tf_op jit(solution)/shard_map/all_to_all | solution.py:85
  73.2 4.8 %all-to-all-start.2 = ((bf16[32,16,1152]{2,1,0:T(8,128)(2,1)}), bf16[32,16,1152]{2,1,0:T(8,128)(2,1)S(1)}, u32[]{:S(2)}, u32[]{:S(2)}) async-start(bf16[32,16,1152]{2,1,0:T(8,128)(2,1)} %pad_maximum_fusion), calls=%async_computation.2 | async-start | bytes 2359296 | tf_op jit(solution)/shard_map/all_to_all | solution.py:88
  78.0 0.0 copy-done.1
  78.0 0.2 copy.35
  78.2 0.0 copy-start.2
  78.3 0.1 copy.36.w_ref
  78.5 0.2 copy.32
  78.7 17.9 %all-to-all-done.2 = bf16[32,16,1152]{2,1,0:T(8,128)(2,1)S(1)} async-done(((bf16[32,16,1152]{2,1,0:T(8,128)(2,1)}), bf16[32,16,1152]{2,1,0:T(8,128)(2,1)S(1)}, u32[]{:S(2)}, u32[]{:S(2)}) %all-to-all-start.2) | async-done | bytes 1179680 | tf_op jit(solution)/shard_map/all_to_all | solution.py:88
  96.6 0.0 copy-done.2
  96.6 0.1 broadcast_in_dim.11.bias_ref
  96.7 3.8 %pair.1 = f32[32,64,128]{2,1,0:T(8,128)} custom-call(bf16[1152,256]{1,0:T(8,128)(2,1)S(1)} %bitcast.24, bf16[2,256,1152]{2,1,0:T(8,128)(2,1)S(1)} %bitcast.23, bf16[256,512]{1,0:T(8,128)(2,1)S(1)} %copy.36.w_ref, f32[128,128]{1,0:T(8,128)S(1)} %broadcast_in_dim.11.bias_ref), custom_call_target="tpu_custom_call" | custom-call | flops 2000000000 | bytes 4194304 | tf_op jit(solution)/shard_map/pair/pallas_call | solution.py:65
  (4 shorter events, 0.1 us)
Async XLA Ops:
  0.0 3.1 %copy-start = (bf16[256,64]{0,1:T(8,128)(2,1)S(1)}, bf16[256,64]{0,1:T(8,128)(2,1)}, u32[]{:S(2)}) copy-start(bf16[256,64]{0,1:T(8,128)(2,1)} %param.14) | copy-start | bytes 98308
  5.9 41.1 %all-to-all-start.1 = ((bf16[16,16,1152]{2,1,0:T(8,128)(2,1)}), bf16[16,16,1152]{2,1,0:T(8,128)(2,1)S(1)}, u32[]{:S(2)}, u32[]{:S(2)}) async-start(bf16[16,16,1152]{2,1,0:T(8,128)(2,1)} %broadcast_in_dim.10), calls=%async_computation.1 | async-start | bytes 1179648 | tf_op jit(solution)/shard_map/all_to_all | solution.py:86
  47.8 25.4 %all-to-all-start = ((bf16[16,16,1152]{2,1,0:T(8,128)(2,1)}), bf16[16,16,1152]{2,1,0:T(8,128)(2,1)S(1)}, u32[]{:S(2)}, u32[]{:S(2)}) async-start(bf16[16,16,1152]{2,1,0:T(8,128)(2,1)} %broadcast_in_dim.9), calls=%async_computation | async-start | bytes 1179648 | tf_op jit(solution)/shard_map/all_to_all | solution.py:85
  62.4 15.6 %copy-start.1 = (bf16[1024,128]{1,0:T(8,128)(2,1)S(1)}, bf16[1024,128]{1,0:T(8,128)(2,1)}, u32[]{:S(2)}) copy-start(bf16[1024,128]{1,0:T(8,128)(2,1)} %param.16) | copy-start | bytes 786436
  73.2 23.4 %all-to-all-start.2 = ((bf16[32,16,1152]{2,1,0:T(8,128)(2,1)}), bf16[32,16,1152]{2,1,0:T(8,128)(2,1)S(1)}, u32[]{:S(2)}, u32[]{:S(2)}) async-start(bf16[32,16,1152]{2,1,0:T(8,128)(2,1)} %pad_maximum_fusion), calls=%async_computation.2 | async-start | bytes 2359296 | tf_op jit(solution)/shard_map/all_to_all | solution.py:88
  78.2 18.3 %copy-start.2 = (f32[128]{0:T(128)S(1)}, f32[128]{0:T(128)}, u32[]{:S(2)}) copy-start(f32[128]{0:T(128)} %param.17) | copy-start | bytes 1540

commit v2 on v1

v2 whole, which is shorter than its diff:
```python
import jax
import jax.numpy as jnp
from jax import lax
from jax.experimental import pallas as pl
from jax.experimental.pallas import tpu as pltpu
from jax.sharding import Mesh, PartitionSpec as P

EPSILON = 1e-05
RES = ("z", "xl")
SEQ = ("y", "xh", "core")


def iota(shape, dim):
    return lax.broadcasted_iota(jnp.int32, shape, dim)


def ones_where(condition, dtype=jnp.bfloat16):
    return jnp.where(condition, 1.0, 0.0).astype(dtype)


def project_kernel(*refs):
    sources, (a_ref, b_ref), held, (pa, tiles, sems) = refs[:7], refs[7:9], refs[9:16], refs[16:]
    loads = [pltpu.make_async_copy(src, dst, sems.at[k]) for k, (src, dst) in enumerate(zip(sources, held))]
    for load in loads:
        load.start()
    for load in loads:
        load.wait()
    x_ref, mask_ref, present_ref, gain_ref, bias_ref, w_ref, pb_ref = held
    value = x_ref[...].reshape(512, 256).astype(jnp.float32)
    mean = jnp.mean(value, axis=-1, keepdims=True)
    centred = value - mean
    var = jnp.mean(centred * centred, axis=-1, keepdims=True)
    normed = (centred * lax.rsqrt(var + EPSILON) * gain_ref[...] + bias_ref[...]).astype(jnp.bfloat16)
    weights = (mask_ref[...] * present_ref[...]).astype(jnp.float32).astype(jnp.bfloat16)
    proj_w = w_ref[...]

    row, col = iota((32, 64), 0), iota((32, 64), 1)
    place = row // 8
    pick = ones_where(col == 32 + 4 * (row % 8) + (place % 2) * 2 + place // 2)
    wb = jnp.dot(pick, proj_w, preferred_element_type=jnp.float32)
    bt = lax.dot_general(wb.astype(jnp.bfloat16), normed, (((1,), (1,)), ((), ())), preferred_element_type=jnp.float32)
    row, col = iota((8, 64), 0), iota((8, 64), 1)
    own = jnp.where((col >= 32) & ((col - 32) // 4 == row), pb_ref[...], 0.0)
    row, lane = iota((64, 128), 0), iota((64, 128), 1) // 32
    spread = ones_where(row % 4 == (lane % 2) * 2 + lane // 2, jnp.float32)
    b_bias = jnp.dot(own, spread, precision=lax.Precision.HIGHEST, preferred_element_type=jnp.float32)
    group = iota((8, 128), 1) // 32
    for t in range(4):
        parts = [bt[p * 8:(p + 1) * 8, t * 128:(t + 1) * 128] for p in range(4)]
        for r in range(4):
            out = parts[r]
            for p in range(4):
                if p != r:
                    out = jnp.where(group == p, pltpu.roll(parts[p], (32 * (p - r)) % 128, 1), out)
            tiles[pl.ds(4 * t + r, 8, stride=16), :] = out + b_bias
    row, lane = iota((32, 128), 0), iota((32, 128), 1)
    b_weights = jnp.dot(weights, ones_where(lane % 32 == row), preferred_element_type=jnp.float32)
    for g in range(8):
        b_ref[g * 16:(g + 1) * 16, :] = (tiles[g * 16:(g + 1) * 16, :] * b_weights).astype(jnp.bfloat16)
    b_plain = jnp.where(iota((16, 128), 1) < 32, b_weights, 0.0)
    b_ref[128:136, :] = (b_plain[:8] + pltpu.roll(b_plain[8:], 64, 1)).astype(jnp.bfloat16)

    row, lane4 = iota((64, 128), 0), iota((64, 128), 1)
    four = ones_where(row == lane4 % 32)
    wa = lax.dot_general(four, proj_w, (((0,), (0,)), ((), ())), preferred_element_type=jnp.float32)
    a_bias = jnp.dot(jnp.broadcast_to(pb_ref[...], (8, 64)), four.astype(jnp.float32),
                     precision=lax.Precision.HIGHEST, preferred_element_type=jnp.float32)
    pa[...] = lax.dot_general(normed, wa.astype(jnp.bfloat16), (((1,), (1,)), ((), ())),
                              preferred_element_type=jnp.float32) + a_bias[0:1]
    group = iota((16, 128), 1) // 32
    for g in range(8):
        part = [pa[pl.ds(4 * g + k, 16, stride=32), :] for k in range(4)]
        out = jnp.where(group < 2, jnp.where(group == 0, part[0], part[1]), jnp.where(group == 2, part[2], part[3]))
        spread = jnp.dot(weights, ones_where(row[:32] == 4 * g + lane // 32), preferred_element_type=jnp.float32)
        a_ref[g * 16:(g + 1) * 16, :] = (out * spread).astype(jnp.bfloat16)
    even_odd = ones_where(lane == (row[:32] % 2) * 16 + row[:32] // 2)
    a_plain = jnp.dot(weights, even_odd, preferred_element_type=jnp.float32)
    a_ref[128:136, :] = (a_plain[:8] + pltpu.roll(a_plain[8:], 64, 1)).astype(jnp.bfloat16)


def project(x, mask, present, gain, bias, weight, proj_bias):
    vmem = pl.BlockSpec(memory_space=pltpu.VMEM)
    out = jax.ShapeDtypeStruct((136, 128), jnp.bfloat16)
    given = (x, mask, present[None], gain[None], bias[None], weight.T, proj_bias[None])
    return pl.pallas_call(
        project_kernel,
        out_shape=(out, out),
        in_specs=[pl.BlockSpec(memory_space=pl.ANY)] * 7,
        out_specs=(vmem, vmem),
        scratch_shapes=[pltpu.VMEM(g.shape, g.dtype) for g in given] + [
            pltpu.VMEM((512, 128), jnp.float32), pltpu.VMEM((128, 128), jnp.float32), pltpu.SemaphoreType.DMA((7,))],
        compiler_params=pltpu.CompilerParams(vmem_limit_bytes=56 * 1024 * 1024),
        cost_estimate=pl.CostEstimate(flops=4 * 10**7, bytes_accessed=2**19, transcendentals=0),
        name="project",
    )(*given)


def rows_kernel(pos_ref, own_ref, other_ref, at_ref, wa_ref, rows, packed):
    for k in range(16):
        src = own_ref if k < 8 else other_ref
        at = pos_ref[k]
        for g in range(8):
            rows[pl.ds(pl.multiple_of(at * 16, 16), 16), g * 128:(g + 1) * 128] = src[k % 8, g * 16:(g + 1) * 16, :]
        packed[pl.ds(pl.multiple_of(at * 8, 8), 8), :] = src[k % 8, 128:136, :].astype(jnp.float32)
    for g in range(8):
        at_ref[g * 128:(g + 1) * 128, :] = rows[:, g * 128:(g + 1) * 128].T
    wa_ref[...] = packed[...].astype(jnp.bfloat16)


def gather_rows(pos, own, other):
    vmem = pl.BlockSpec(memory_space=pltpu.VMEM)
    return pl.pallas_call(
        rows_kernel,
        out_shape=(jax.ShapeDtypeStruct((1024, 256), jnp.bfloat16), jax.ShapeDtypeStruct((128, 128), jnp.bfloat16)),
        in_specs=[pl.BlockSpec(memory_space=pltpu.SMEM), vmem, vmem],
        out_specs=(vmem, vmem),
        scratch_shapes=[pltpu.VMEM((256, 1024), jnp.bfloat16), pltpu.VMEM((128, 128), jnp.float32)],
        compiler_params=pltpu.CompilerParams(vmem_limit_bytes=16 * 1024 * 1024),
        cost_estimate=pl.CostEstimate(flops=10**6, bytes_accessed=2 * 2**20, transcendentals=0),
        name="rows",
    )(pos, own, other)


def pair_kernel(at_ref, wa_ref, b_ref, w_ref, bias_ref, o_ref, bint, xs):
    lane = iota((256, 128), 1)
    odd = (lane // 32) % 2 == 1
    for g in range(8):
        v0 = b_ref[0, :, g * 16:(g + 1) * 16, :].reshape(256, 128).astype(jnp.float32)
        v1 = b_ref[1, :, g * 16:(g + 1) * 16, :].reshape(256, 128).astype(jnp.float32)
        bint[:, (2 * g) * 128:(2 * g + 1) * 128] = jnp.where(odd, pltpu.roll(v1, 32, 1), v0).astype(jnp.bfloat16)
        bint[:, (2 * g + 1) * 128:(2 * g + 2) * 128] = jnp.where(odd, v1, pltpu.roll(v0, 96, 1)).astype(jnp.bfloat16)
    w0 = b_ref[0, :, 128:136, :].astype(jnp.float32).reshape(128, 128)
    w1 = b_ref[1, :, 128:136, :].astype(jnp.float32).reshape(128, 128)
    wb = (w0 + pltpu.roll(w1, 32, 1)).astype(jnp.bfloat16)
    count = lax.dot_general(wa_ref[...], wb, (((0,), (0,)), ((), ())), preferred_element_type=jnp.float32)
    count = count[0:32] + pltpu.roll(count[64:96], 64, 1)
    low = lax.broadcasted_iota(jnp.int32, (16, 128), 1) < 64
    inv = 1.0 / jnp.maximum(jnp.where(low, count[:16], pltpu.roll(count[16:], 64, 1)), 1.0)
    bias = bias_ref[...]
    low = lane[:128] < 64
    for n in range(8):
        for m in range(4):
            o = jnp.dot(at_ref[m * 256:(m + 1) * 256, :], bint[:, n * 256:(n + 1) * 256],
                        preferred_element_type=jnp.float32).astype(jnp.bfloat16)
            for k in range(8):
                i = m * 8 + k
                for t in range(2):
                    h = 2 * n + t
                    xs[i // 2, h * 32:(h + 1) * 32, (i % 2) * 128:(i % 2 + 1) * 128] = (
                        o[k * 32:(k + 1) * 32, t * 128:(t + 1) * 128])
    for ip in range(16):
        y = jnp.dot(w_ref[...], xs[ip], preferred_element_type=jnp.float32)
        t0, b0, t1, b1 = y[:128, :128], y[128:, :128], y[:128, 128:], y[128:, 128:]
        u = jnp.where(low, t0, b1)
        v = jnp.where(low, t1, b0)
        z = (u + pltpu.roll(v, 64, 1) + bias) * inv[ip:ip + 1]
        zt = z.T
        o_ref[2 * ip] = zt[:64]
        o_ref[2 * ip + 1] = zt[64:]


def pair(at, wa, b, w2, bias):
    return pl.pallas_call(
        pair_kernel,
        out_shape=jax.ShapeDtypeStruct((32, 64, 128), jnp.float32),
        in_specs=[pl.BlockSpec(memory_space=pltpu.VMEM)] * 5,
        out_specs=pl.BlockSpec(memory_space=pltpu.VMEM),
        scratch_shapes=[pltpu.VMEM((256, 2048), jnp.bfloat16), pltpu.VMEM((16, 512, 256), jnp.bfloat16)],
        compiler_params=pltpu.CompilerParams(vmem_limit_bytes=40 * 1024 * 1024),
        cost_estimate=pl.CostEstimate(flops=2 * 10**9, bytes_accessed=4 * 2**20, transcendentals=0),
        name="pair",
    )(at, wa, b, w2, bias)


def shift(n, by):
    return [(i, (i + by) % n) for i in range(n)]


def local(x, mask, present, gain, bias, weight, proj_bias, out_weight, out_bias):
    a, b = project(x, mask, present, gain, bias, weight, proj_bias)
    ax = lax.ppermute(a, "xh", shift(2, 1))
    b_z = lax.all_gather(b, "z")
    b_z, ax = lax.optimization_barrier((b_z, ax))
    b_two = jnp.broadcast_to(b_z[None], (2, *b_z.shape)).reshape(32, 136, 128)
    b_all = lax.all_to_all(b_two, ("xl",) + SEQ, 0, 0, tiled=True).reshape(2, 16, 136, 128)

    ay = [jnp.stack([a, ax])]
    for _ in range(3):
        ay.append(lax.ppermute(ay[-1], "y", shift(4, -1)))
    mine = jnp.concatenate(ay)
    other = lax.ppermute(mine, "core", shift(2, 1))
    y, xh, core = (lax.axis_index(n) for n in SEQ)
    pos = jnp.stack([
        ((y + k) % 4) * 4 + (xh ^ h) * 2 + (core ^ c) for c in range(2) for k in range(4) for h in range(2)
    ]).astype(jnp.int32)
    at, wa = gather_rows(pos, mine, other)

    w2 = out_weight.reshape(32, 16, 2, 128).transpose(2, 3, 1, 0).reshape(256, 512)
    bias2 = jnp.broadcast_to(out_bias[:, None], (128, 128))
    return pair(at, wa, b_all, w2, bias2)


def solution(mesh):
    fine = Mesh(mesh.devices.reshape(16, 2, 4, 2, 2), RES + SEQ)
    in_specs = (P(SEQ, RES, None), P(SEQ, RES), P(RES), P(), P(), P(), P(), P(), P())
    return jax.shard_map(local, mesh=fine, in_specs=in_specs, out_specs=P(RES, SEQ, None), check_vma=False)
```

time: 101 us -> 92.1 us (0.912)
  the two profiles are of different devices: /device:TPU:1 before, /device:TPU:27 now
where the time goes in v2:
time: 92.1 us; the launch traced here: 91.7 us
  blocking collectives  32.2 us (35%)
  starting transfers between devices  29 us (31%)
  waiting for transfers between devices  21.3 us (23%)
  Pallas kernels  7.15 us (8%)
  local copies, waits for them, and re-layouts  1.8 us (2%)
    all_gather x1, blocking collectives, local(): b_z = lax.all_gather(b, 'z')  32.2 us
    ppermute x3, waiting for transfers between devices, local(): ay.append(lax.ppermute(ay[-1], 'y', shift(4, -1)))  20.8 us
    all_to_all x1, starting transfers between devices, local(): lax.all_to_all(b_two, ('xl',) + SEQ, 0, 0, tiled=True)  13.8 us
    ppermute x3, starting transfers between devices, local(): ay.append(lax.ppermute(ay[-1], 'y', shift(4, -1)))  6.89 us
    ppermute x1, starting transfers between devices, local(): other = lax.ppermute(mine, 'core', shift(2, 1))  4.6 us
    pallas_call x1, Pallas kernels, pair(): pl.pallas_call(pair_kernel, out_shape=jax.ShapeDtypeStruct((32, 64, 128),...  3.81 us
    ppermute x1, starting transfers between devices, local(): ax = lax.ppermute(a, 'xh', shift(2, 1))  3.75 us
    pallas_call x1, Pallas kernels, project(): pl.pallas_call(project_kernel, out_shape=(out, out), in_specs=[pl.BlockSp...  2.5 us
  transfers between devices with their start and end apart: 6, of which 4 were waited for; matrix products, arithmetic and copies ran while one was open for 1% of the time, Pallas kernels for 1%

profile of v2, /device:TPU:27, one launch (start us, length us, event | category | flops | bytes accessed | tf_op | source)
XLA Modules:
  0.0 91.7 jit_solution(3416900294828195679)
XLA Ops:
  0.0 2.5 %project.1 = (bf16[136,128]{1,0:T(8,128)(2,1)}, bf16[136,128]{1,0:T(8,128)(2,1)}) custom-call(bf16[16,32,256]{2,1,0:T(8,128)(2,1)} %refs_0_.1, s32[16,32]{1,0:T(8,128)} %refs_1_.1, s32[1,32]{1,0:T(1,128)} %bitcast.47, f32[1,256]{1,0:T(1,128)} %bitcast.45, f32[1,256]{1,0:T(1,128)} %bitcast.46, bf16[64,256]{1,0:T(8,128)(2,1)} %bitcast.44, f32[1,64]{1,0:T(1,128)} %bitcast.48), custom_call_target="tpu_custom_call" | custom-call | flops 40000000 | bytes 524288 | tf_op jit(solution)/shard_map/project/pallas_call | solution.py:85
  2.5 3.8 %collective-permute-start = (bf16[136,128]{1,0:T(8,128)(2,1)}, bf16[136,128]{1,0:T(8,128)(2,1)S(1)}, u32[]{:S(2)}, u32[]{:S(2)}) collective-permute-start(bf16[136,128]{1,0:T(8,128)(2,1)} %get-tuple-element.11), channel_id=1, source_target_pairs={{0,2},{2,0},{1,3},{3,1},{4,6},{6,4},{5,7},{7,5},{8,10},{10,8},{9,1... | collective-permute-start | bytes 104456 | tf_op jit(solution)/shard_map/ppermute | solution.py:181
  6.3 32.2 %all-gather = bf16[2176,128]{1,0:T(8,128)(2,1)S(1)} all-gather(bf16[136,128]{1,0:T(8,128)(2,1)} %get-tuple-element.12), channel_id=2, replica_groups=mesh['z'=16,'xl'=2,'y'=4,'xh'=2,'core'=2] {'z'}, dimensions={0}, use_global_device_ids=true | all-gather | bytes 591872 | tf_op jit(solution)/shard_map/all_gather | solution.py:182
  38.5 0.0 collective-permute-done
  38.5 1.1 %broadcast_in_dim.28 = bf16[2,16,136,128]{3,2,1,0:T(8,128)(2,1)} broadcast(bf16[16,136,128]{2,1,0:T(8,128)(2,1)S(1)} %bitcast.38), dimensions={1,2,3} | broadcast | bytes 1671168 | tf_op jit(solution)/shard_map/broadcast_in_dim | solution.py:184
  39.6 0.0 copy-start.1
  39.6 0.0 copy-start
  39.6 13.8 %all-to-all-start = ((bf16[32,136,128]{2,1,0:T(8,128)(2,1)}), bf16[32,136,128]{2,1,0:T(8,128)(2,1)S(1)}, u32[]{:S(2)}, u32[]{:S(2)}) async-start(bf16[32,136,128]{2,1,0:T(8,128)(2,1)} %bitcast.24), calls=%async_computation | async-start | bytes 2228224 | tf_op jit(solution)/shard_map/all_to_all | solution.py:185
  53.4 0.0 copy-done.1
  53.5 2.5 %collective-permute-start.1 = (bf16[2,136,128]{2,1,0:T(8,128)(2,1)S(1)}, bf16[2,136,128]{2,1,0:T(8,128)(2,1)S(1)}, u32[]{:S(2)}, u32[]{:S(2)}) collective-permute-start(bf16[2,136,128]{2,1,0:T(8,128)(2,1)S(1)} %pad_maximum_fusion), channel_id=1, source_target_pairs={{0,12},{4,0},{8,4},{12,8},{1,13},{5,1},{9,5},{13,9},{2,14},{6,2},{... | collective-permute-start | bytes 208904 | tf_op jit(solution)/shard_map/ppermute | solution.py:189
  56.0 12.7 %collective-permute-done.1 = bf16[2,136,128]{2,1,0:T(8,128)(2,1)S(1)} collective-permute-done((bf16[2,136,128]{2,1,0:T(8,128)(2,1)S(1)}, bf16[2,136,128]{2,1,0:T(8,128)(2,1)S(1)}, u32[]{:S(2)}, u32[]{:S(2)}) %collective-permute-start.1) | collective-permute-done | bytes 69664 | tf_op jit(solution)/shard_map/ppermute | solution.py:189
  68.7 2.5 %collective-permute-start.2 = (bf16[2,136,128]{2,1,0:T(8,128)(2,1)S(1)}, bf16[2,136,128]{2,1,0:T(8,128)(2,1)S(1)}, u32[]{:S(2)}, u32[]{:S(2)}) collective-permute-start(bf16[2,136,128]{2,1,0:T(8,128)(2,1)S(1)} %collective-permute-done.1), channel_id=1, source_target_pairs={{0,12},{4,0},{8,4},{12,8},{1,13},{5,1},{9,5},{13,9},{2,14},{6,2},{... | collective-permute-start | bytes 208904 | tf_op jit(solution)/shard_map/ppermute | solution.py:189
  71.3 3.7 %collective-permute-done.2 = bf16[2,136,128]{2,1,0:T(8,128)(2,1)S(1)} collective-permute-done((bf16[2,136,128]{2,1,0:T(8,128)(2,1)S(1)}, bf16[2,136,128]{2,1,0:T(8,128)(2,1)S(1)}, u32[]{:S(2)}, u32[]{:S(2)}) %collective-permute-start.2) | collective-permute-done | bytes 69664 | tf_op jit(solution)/shard_map/ppermute | solution.py:189
  75.0 1.9 %collective-permute-start.3 = (bf16[2,136,128]{2,1,0:T(8,128)(2,1)S(1)}, bf16[2,136,128]{2,1,0:T(8,128)(2,1)S(1)}, u32[]{:S(2)}, u32[]{:S(2)}) collective-permute-start(bf16[2,136,128]{2,1,0:T(8,128)(2,1)S(1)} %collective-permute-done.2), channel_id=1, source_target_pairs={{0,12},{4,0},{8,4},{12,8},{1,13},{5,1},{9,5},{13,9},{2,14},{6,2},{... | collective-permute-start | bytes 208904 | tf_op jit(solution)/shard_map/ppermute | solution.py:189
  76.9 4.3 %collective-permute-done.3 = bf16[2,136,128]{2,1,0:T(8,128)(2,1)S(1)} collective-permute-done((bf16[2,136,128]{2,1,0:T(8,128)(2,1)S(1)}, bf16[2,136,128]{2,1,0:T(8,128)(2,1)S(1)}, u32[]{:S(2)}, u32[]{:S(2)}) %collective-permute-start.3) | collective-permute-done | bytes 69664 | tf_op jit(solution)/shard_map/ppermute | solution.py:189
  81.2 4.6 %collective-permute-start.4 = (bf16[8,136,128]{2,1,0:T(8,128)(2,1)S(1)}, bf16[8,136,128]{2,1,0:T(8,128)(2,1)S(1)}, u32[]{:S(2)}, u32[]{:S(2)}) collective-permute-start(bf16[8,136,128]{2,1,0:T(8,128)(2,1)S(1)} %constant_dynamic-update-slice_fusion.own_ref), channel_id=1, source_target_pairs={{0,1},{1,0},{2,3},{3,2},{4,5},{5,4},{6,7},{7,6},{8,9},{9,8},{10,11... | collective-permute-start | bytes 835592 | tf_op jit(solution)/shard_map/ppermute | solution.py:191
  85.9 0.0 copy-start.2
  85.9 0.0 copy-done
  85.9 0.2 copy.11
  86.2 0.1 copy.12.w_ref
  86.3 0.1 stack.76.pos_ref
  86.4 0.5 collective-permute-done.4.other_ref
  87.0 0.8 rows.1
  87.8 0.0 all-to-all-done
  87.8 0.0 copy-done.2
  87.9 0.1 broadcast_in_dim.29.bias_ref
  87.9 3.8 %pair.1 = f32[32,64,128]{2,1,0:T(8,128)} custom-call(bf16[1024,256]{1,0:T(8,128)(2,1)S(1)} %get-tuple-element.14.at_ref, bf16[128,128]{1,0:T(8,128)(2,1)S(1)} %get-tuple-element.15.wa_ref, bf16[2,16,136,128]{3,2,1,0:T(8,128)(2,1)S(1)} %bitcast.37, bf16[256,512]{1,0:T(8,128)(2,1)S(1)} %copy.12.w_ref, f32[128,128]{1,0:T(8,128)S(1)} %broadcast_in_dim.29.bias_ref), custom_call_target="tpu_custom_call" | custom-call | flops 2000000000 | bytes 4194304 | tf_op jit(solution)/shard_map/pair/pallas_call | solution.py:163
  (7 shorter events, 0.1 us)
Async XLA Ops:
  2.5 36.0 %collective-permute-start = (bf16[136,128]{1,0:T(8,128)(2,1)}, bf16[136,128]{1,0:T(8,128)(2,1)S(1)}, u32[]{:S(2)}, u32[]{:S(2)}) collective-permute-start(bf16[136,128]{1,0:T(8,128)(2,1)} %get-tuple-element.11), channel_id=1, source_target_pairs={{0,2},{2,0},{1,3},{3,1},{4,6},{6,4},{5,7},{7,5},{8,10},{10,8},{9,1... | collective-permute-start | bytes 104456 | tf_op jit(solution)/shard_map/ppermute | solution.py:181
  39.6 13.8 %copy-start.1 = (bf16[136,128]{1,0:T(8,128)(2,1)S(1)}, bf16[136,128]{1,0:T(8,128)(2,1)}, u32[]{:S(2)}) copy-start(bf16[136,128]{1,0:T(8,128)(2,1)} %get-tuple-element.11) | copy-start | bytes 104452
  39.6 46.3 %copy-start = (bf16[1024,128]{1,0:T(8,128)(2,1)S(1)}, bf16[1024,128]{1,0:T(8,128)(2,1)}, u32[]{:S(2)}) copy-start(bf16[1024,128]{1,0:T(8,128)(2,1)} %param.16) | copy-start | bytes 786436
  39.6 48.2 %all-to-all-start = ((bf16[32,136,128]{2,1,0:T(8,128)(2,1)}), bf16[32,136,128]{2,1,0:T(8,128)(2,1)S(1)}, u32[]{:S(2)}, u32[]{:S(2)}) async-start(bf16[32,136,128]{2,1,0:T(8,128)(2,1)} %bitcast.24), calls=%async_computation | async-start | bytes 2228224 | tf_op jit(solution)/shard_map/all_to_all | solution.py:185
  53.5 15.2 %collective-permute-start.1 = (bf16[2,136,128]{2,1,0:T(8,128)(2,1)S(1)}, bf16[2,136,128]{2,1,0:T(8,128)(2,1)S(1)}, u32[]{:S(2)}, u32[]{:S(2)}) collective-permute-start(bf16[2,136,128]{2,1,0:T(8,128)(2,1)S(1)} %pad_maximum_fusion), channel_id=1, source_target_pairs={{0,12},{4,0},{8,4},{12,8},{1,13},{5,1},{9,5},{13,9},{2,14},{6,2},{... | collective-permute-start | bytes 208904 | tf_op jit(solution)/shard_map/ppermute | solution.py:189
  68.7 6.3 %collective-permute-start.2 = (bf16[2,136,128]{2,1,0:T(8,128)(2,1)S(1)}, bf16[2,136,128]{2,1,0:T(8,128)(2,1)S(1)}, u32[]{:S(2)}, u32[]{:S(2)}) collective-permute-start(bf16[2,136,128]{2,1,0:T(8,128)(2,1)S(1)} %collective-permute-done.1), channel_id=1, source_target_pairs={{0,12},{4,0},{8,4},{12,8},{1,13},{5,1},{9,5},{13,9},{2,14},{6,2},{... | collective-permute-start | bytes 208904 | tf_op jit(solution)/shard_map/ppermute | solution.py:189
  75.0 6.3 %collective-permute-start.3 = (bf16[2,136,128]{2,1,0:T(8,128)(2,1)S(1)}, bf16[2,136,128]{2,1,0:T(8,128)(2,1)S(1)}, u32[]{:S(2)}, u32[]{:S(2)}) collective-permute-start(bf16[2,136,128]{2,1,0:T(8,128)(2,1)S(1)} %collective-permute-done.2), channel_id=1, source_target_pairs={{0,12},{4,0},{8,4},{12,8},{1,13},{5,1},{9,5},{13,9},{2,14},{6,2},{... | collective-permute-start | bytes 208904 | tf_op jit(solution)/shard_map/ppermute | solution.py:189
  81.2 5.8 %collective-permute-start.4 = (bf16[8,136,128]{2,1,0:T(8,128)(2,1)S(1)}, bf16[8,136,128]{2,1,0:T(8,128)(2,1)S(1)}, u32[]{:S(2)}, u32[]{:S(2)}) collective-permute-start(bf16[8,136,128]{2,1,0:T(8,128)(2,1)S(1)} %constant_dynamic-update-slice_fusion.own_ref), channel_id=1, source_target_pairs={{0,1},{1,0},{2,3},{3,2},{4,5},{5,4},{6,7},{7,6},{8,9},{9,8},{10,11... | collective-permute-start | bytes 835592 | tf_op jit(solution)/shard_map/ppermute | solution.py:191
  85.9 2.0 %copy-start.2 = (f32[128]{0:T(128)S(1)}, f32[128]{0:T(128)}, u32[]{:S(2)}) copy-start(f32[128]{0:T(128)} %param.17) | copy-start | bytes 1540

commit v3 on v2

v3 whole, which is shorter than its diff:
```python
import jax
import jax.numpy as jnp
from jax import lax
from jax.experimental import pallas as pl
from jax.experimental.pallas import tpu as pltpu
from jax.sharding import Mesh, PartitionSpec as P

EPSILON = 1e-05
RES = ("z", "xl")
SEQ = ("y", "xh", "core")


def iota(shape, dim):
    return lax.broadcasted_iota(jnp.int32, shape, dim)


def ones_where(condition, dtype=jnp.bfloat16):
    return jnp.where(condition, 1.0, 0.0).astype(dtype)


def project_kernel(*refs):
    sources, (a_ref, b_ref), held, (pa, tiles, sems) = refs[:7], refs[7:9], refs[9:16], refs[16:]
    loads = [pltpu.make_async_copy(src, dst, sems.at[k]) for k, (src, dst) in enumerate(zip(sources, held))]
    for load in loads:
        load.start()
    for load in loads:
        load.wait()
    x_ref, mask_ref, present_ref, gain_ref, bias_ref, w_ref, pb_ref = held
    value = x_ref[...].reshape(512, 256).astype(jnp.float32)
    mean = jnp.mean(value, axis=-1, keepdims=True)
    centred = value - mean
    var = jnp.mean(centred * centred, axis=-1, keepdims=True)
    normed = (centred * lax.rsqrt(var + EPSILON) * gain_ref[...] + bias_ref[...]).astype(jnp.bfloat16)
    weights = (mask_ref[...] * present_ref[...]).astype(jnp.float32).astype(jnp.bfloat16)
    proj_w = w_ref[...]

    row, col = iota((32, 64), 0), iota((32, 64), 1)
    pick = ones_where(col == 32 + 4 * (row % 8) + row // 8)
    wb = jnp.dot(pick, proj_w, preferred_element_type=jnp.float32)
    bt = lax.dot_general(wb.astype(jnp.bfloat16), normed, (((1,), (1,)), ((), ())), preferred_element_type=jnp.float32)
    row, col = iota((8, 64), 0), iota((8, 64), 1)
    own = jnp.where((col >= 32) & ((col - 32) // 4 == row), pb_ref[...], 0.0)
    row, lane = iota((64, 128), 0), iota((64, 128), 1) // 32
    spread = ones_where(row % 4 == lane, jnp.float32)
    b_bias = jnp.dot(own, spread, precision=lax.Precision.HIGHEST, preferred_element_type=jnp.float32)
    group = iota((8, 128), 1) // 32
    for t in range(4):
        parts = [bt[p * 8:(p + 1) * 8, t * 128:(t + 1) * 128] for p in range(4)]
        for r in range(4):
            out = parts[r]
            for p in range(4):
                if p != r:
                    out = jnp.where(group == p, pltpu.roll(parts[p], (32 * (p - r)) % 128, 1), out)
            tiles[pl.ds(4 * t + r, 8, stride=16), :] = out + b_bias
    row, lane = iota((32, 128), 0), iota((32, 128), 1)
    b_weights = jnp.dot(weights, ones_where(lane % 32 == row), preferred_element_type=jnp.float32)
    for g in range(8):
        b_ref[g * 16:(g + 1) * 16, :] = (tiles[g * 16:(g + 1) * 16, :] * b_weights).astype(jnp.bfloat16)
    b_plain = jnp.where(iota((16, 128), 1) < 32, b_weights, 0.0)
    b_ref[128:136, :] = (b_plain[:8] + pltpu.roll(b_plain[8:], 64, 1)).astype(jnp.bfloat16)

    row, lane4 = iota((64, 128), 0), iota((64, 128), 1)
    four = ones_where(row == lane4 % 32)
    wa = lax.dot_general(four, proj_w, (((0,), (0,)), ((), ())), preferred_element_type=jnp.float32)
    a_bias = jnp.dot(jnp.broadcast_to(pb_ref[...], (8, 64)), four.astype(jnp.float32),
                     precision=lax.Precision.HIGHEST, preferred_element_type=jnp.float32)
    pa[...] = lax.dot_general(normed, wa.astype(jnp.bfloat16), (((1,), (1,)), ((), ())),
                              preferred_element_type=jnp.float32) + a_bias[0:1]
    group = iota((16, 128), 1) // 32
    for g in range(8):
        part = [pa[pl.ds(4 * g + k, 16, stride=32), :] for k in range(4)]
        out = jnp.where(group < 2, jnp.where(group == 0, part[0], part[1]), jnp.where(group == 2, part[2], part[3]))
        spread = jnp.dot(weights, ones_where(row[:32] == 4 * g + lane // 32), preferred_element_type=jnp.float32)
        a_ref[g * 16:(g + 1) * 16, :] = (out * spread).astype(jnp.bfloat16)
    by_four = ones_where(iota((32, 128), 1) == (row[:32] % 4) * 8 + row[:32] // 4)
    a_plain = jnp.dot(weights, by_four, preferred_element_type=jnp.float32)
    a_ref[128:136, :] = (a_plain[:8] + pltpu.roll(a_plain[8:], 64, 1)).astype(jnp.bfloat16)


def project(x, mask, present, gain, bias, weight, proj_bias):
    vmem = pl.BlockSpec(memory_space=pltpu.VMEM)
    out = [jax.ShapeDtypeStruct((136, 128), jnp.bfloat16)] * 2
    given = (x, mask, present[None], gain[None], bias[None], weight.T, proj_bias[None])
    return pl.pallas_call(
        project_kernel,
        out_shape=out,
        in_specs=[pl.BlockSpec(memory_space=pl.ANY)] * 7,
        out_specs=[vmem, vmem],
        scratch_shapes=[pltpu.VMEM(g.shape, g.dtype) for g in given] + [
            pltpu.VMEM((512, 128), jnp.float32), pltpu.VMEM((128, 128), jnp.float32), pltpu.SemaphoreType.DMA((7,))],
        compiler_params=pltpu.CompilerParams(vmem_limit_bytes=56 * 1024 * 1024),
        cost_estimate=pl.CostEstimate(flops=4 * 10**7, bytes_accessed=2**19, transcendentals=0),
        name="project",
    )(*given)


def fan_kernel(a_ref, o_ref, held, sems):
    load = pltpu.make_async_copy(a_ref, held, sems.at[32])
    load.start()
    load.wait()
    copies = [pltpu.make_async_copy(held, o_ref.at[k], sems.at[k]) for k in range(32)]
    for copy in copies:
        copy.start()
    for copy in copies:
        copy.wait()


def fan(a):
    return pl.pallas_call(
        fan_kernel,
        out_shape=jax.ShapeDtypeStruct((32, 136, 128), jnp.bfloat16),
        in_specs=[pl.BlockSpec(memory_space=pl.ANY)],
        out_specs=pl.BlockSpec(memory_space=pl.ANY),
        scratch_shapes=[pltpu.VMEM((136, 128), jnp.bfloat16), pltpu.SemaphoreType.DMA((33,))],
        compiler_params=pltpu.CompilerParams(vmem_limit_bytes=56 * 1024 * 1024),
        cost_estimate=pl.CostEstimate(flops=10**9, bytes_accessed=2**21, transcendentals=0),
        name="fan",
    )(a)


def columns_kernel(b_ref, o_ref, wb_ref):
    for g in range(8):
        o_ref[:, g * 128:(g + 1) * 128] = b_ref[:, g * 16:(g + 1) * 16, :].reshape(256, 128)
    wb_ref[...] = b_ref[:, 128:136, :].astype(jnp.float32).reshape(128, 128).astype(jnp.bfloat16)


def columns(b_all):
    vmem = pl.BlockSpec(memory_space=pltpu.VMEM)
    return pl.pallas_call(
        columns_kernel,
        out_shape=[jax.ShapeDtypeStruct(shape, jnp.bfloat16) for shape in ((256, 1024), (128, 128))],
        in_specs=[vmem],
        out_specs=[vmem, vmem],
        compiler_params=pltpu.CompilerParams(vmem_limit_bytes=16 * 1024 * 1024),
        cost_estimate=pl.CostEstimate(flops=10**12, bytes_accessed=2**21, transcendentals=0),
        name="columns",
    )(b_all)


def tile(block, a_ref, b_ref, wb_ref, w_ref, bias_ref, at, xs, put):
    lane = iota((128, 128), 1)
    for g in range(8):
        at[g * 128:(g + 1) * 128, :] = a_ref[block, :, g * 16:(g + 1) * 16, :].reshape(256, 128).T
    wa = a_ref[block, :, 128:136, :].astype(jnp.float32).reshape(128, 128).astype(jnp.bfloat16)
    count = lax.dot_general(wa, wb_ref[...], (((0,), (0,)), ((), ())), preferred_element_type=jnp.float32)
    count = jnp.where(lane[:32] < 32, count[0:32] + pltpu.roll(count[64:96], 64, 1), 0.0)
    spread = count[0:8]
    for k in range(1, 4):
        spread += pltpu.roll(count[k * 8:(k + 1) * 8], 32 * k, 1)
    inv = 1.0 / jnp.maximum(spread, 1.0)
    bias = bias_ref[...]
    group = lane // 32
    for n in range(4):
        for m in range(4):
            o = jnp.dot(at[m * 256:(m + 1) * 256, :], b_ref[:, n * 256:(n + 1) * 256],
                        preferred_element_type=jnp.float32).astype(jnp.bfloat16)
            for k in range(8):
                i = m * 8 + k
                for t in range(2):
                    g = 2 * n + t
                    xs[i // 2, g * 32:(g + 1) * 32, (i % 2) * 128:(i % 2 + 1) * 128] = (
                        o[k * 32:(k + 1) * 32, t * 128:(t + 1) * 128])
    for q in range(8):
        y = [jnp.dot(w_ref[...], xs[2 * q + h], preferred_element_type=jnp.float32) for h in range(2)]
        part = [[y[i // 2][p * 128:(p + 1) * 128, (i % 2) * 128:(i % 2 + 1) * 128] for p in range(4)] for i in range(4)]
        z = bias
        for d in range(4):
            v = [part[(p + d) % 4][p] for p in range(4)]
            v = jnp.where(group < 2, jnp.where(group == 0, v[0], v[1]), jnp.where(group == 2, v[2], v[3]))
            z = z + (pltpu.roll(v, 32 * d, 1) if d else v)
        put(4 * q, (z * inv[q:q + 1]).T)


def foreign_kernel(xl_ref, a_ref, b_ref, wb_ref, w_ref, bias_ref, o_ref, at, xs):
    def put(i, z):
        o_ref[i:i + 4] = z.astype(jnp.bfloat16).reshape(4, 32, 128)

    tile(1 - xl_ref[0], a_ref, b_ref, wb_ref, w_ref, bias_ref, at, xs, put)


def own_kernel(xl_ref, a_ref, b_ref, wb_ref, w_ref, bias_ref, o_ref, at, xs, held, sem):
    def put(i, z):
        held[i:i + 4] = z.reshape(4, 32, 128)

    tile(xl_ref[0], a_ref, b_ref, wb_ref, w_ref, bias_ref, at, xs, put)
    copy = pltpu.make_async_copy(held, o_ref.at[:, pl.ds(pl.multiple_of(xl_ref[0] * 32, 32), 32), :], sem)
    copy.start()
    copy.wait()


def join_kernel(xl_ref, t_ref, given_ref, o_ref, held, sem):
    del given_ref
    held[...] = t_ref[...].astype(jnp.float32)
    copy = pltpu.make_async_copy(held, o_ref.at[:, pl.ds(pl.multiple_of((1 - xl_ref[0]) * 32, 32), 32), :], sem)
    copy.start()
    copy.wait()


def call(kernel, name, shape, dtype, out_space, scratch, flops, in_specs, aliases, args):
    return pl.pallas_call(
        kernel,
        out_shape=jax.ShapeDtypeStruct(shape, dtype),
        in_specs=in_specs,
        out_specs=pl.BlockSpec(memory_space=out_space),
        scratch_shapes=scratch,
        input_output_aliases=aliases,
        compiler_params=pltpu.CompilerParams(vmem_limit_bytes=24 * 1024 * 1024),
        cost_estimate=pl.CostEstimate(flops=flops, bytes_accessed=2**21, transcendentals=0),
        name=name,
    )(*args)


def shift(n, by):
    return [(i, (i + by) % n) for i in range(n)]


def local(x, mask, present, gain, bias, weight, proj_bias, out_weight, out_bias):
    a, b = project(x, mask, present, gain, bias, weight, proj_bias)
    turn = [((z * 2 + xl) * 16 + q, (q * 2 + xl) * 16 + z) for z in range(16) for xl in range(2) for q in range(16)]
    b = lax.ppermute(b, RES + SEQ, turn)
    w4 = out_weight.reshape(32, 8, 4, 128).transpose(2, 3, 1, 0).reshape(512, 256)
    a_all = lax.all_to_all(fan(a), ("xl",) + SEQ, 0, 0, tiled=True).reshape(2, 16, 136, 128)
    b_all = lax.all_gather(b, "z")
    b_all, wb = columns(b_all)
    a_all, b_all, wb = lax.optimization_barrier((a_all, b_all, wb))

    bias2 = jnp.broadcast_to(out_bias[:, None], (128, 128))
    xl = lax.axis_index("xl").astype(jnp.int32).reshape(1)
    smem, vmem, anywhere = (pl.BlockSpec(memory_space=m) for m in (pltpu.SMEM, pltpu.VMEM, pl.ANY))
    work = [pltpu.VMEM((1024, 256), jnp.bfloat16), pltpu.VMEM((16, 256, 256), jnp.bfloat16)]
    held = [pltpu.VMEM((32, 32, 128), jnp.float32), pltpu.SemaphoreType.DMA]
    args, specs = (xl, a_all, b_all, wb, w4, bias2), [smem] + [vmem] * 5
    sent = call(foreign_kernel, "foreign", (32, 32, 128), jnp.bfloat16, pltpu.VMEM, work, 10**9, specs, {}, args)
    taken = lax.ppermute(sent, "xl", shift(2, 1))
    out = call(own_kernel, "own", (32, 64, 128), jnp.float32, pl.ANY, work + held, 10**9, specs, {}, args)
    return call(join_kernel, "join", (32, 64, 128), jnp.float32, pl.ANY, held, 10**6, [smem, vmem, anywhere], {2: 0},
                (xl, taken, out))


def solution(mesh):
    fine = Mesh(mesh.devices.reshape(16, 2, 4, 2, 2), RES + SEQ)
    in_specs = (P(SEQ, RES, None), P(SEQ, RES), P(RES), P(), P(), P(), P(), P(), P())
    return jax.shard_map(local, mesh=fine, in_specs=in_specs, out_specs=P(RES, SEQ, None), check_vma=False)
```

time: 92.1 us -> 72.2 us (0.78)
  the two profiles are of different devices: /device:TPU:27 before, /device:TPU:14 now
where the time goes in v3:
time: 72.2 us; the launch traced here: 71.8 us
  blocking collectives  30.8 us (43%)
  starting transfers between devices  25.2 us (35%)
  Pallas kernels  13 us (18%)
  waiting for transfers between devices  1.84 us (3%)
  local copies, waits for them, and re-layouts  0.84 us (1%)
    all_gather x1, blocking collectives, local(): b_all = lax.all_gather(b, 'z')  30.8 us
    ppermute x1, starting transfers between devices, local(): b = lax.ppermute(b, RES + SEQ, turn)  12.5 us
    all_to_all x1, starting transfers between devices, local(): lax.all_to_all(fan(a), ('xl',) + SEQ, 0, 0, tiled=True)  10.3 us
    pallas_call x3, Pallas kernels, call(): pl.pallas_call(kernel, out_shape=jax.ShapeDtypeStruct(shape, dtype), in_s...  8.25 us
    pallas_call x1, Pallas kernels, project(): pl.pallas_call(project_kernel, out_shape=out, in_specs=[pl.BlockSpec(memo...  2.5 us
    ppermute x1, starting transfers between devices, local(): taken = lax.ppermute(sent, 'xl', shift(2, 1))  2.3 us
    pallas_call x1, Pallas kernels, fan(): pl.pallas_call(fan_kernel, out_shape=jax.ShapeDtypeStruct((32, 136, 128),...  2.08 us
    ppermute x1, waiting for transfers between devices, local(): taken = lax.ppermute(sent, 'xl', shift(2, 1))  1.84 us
  transfers between devices with their start and end apart: 3, of which 1 were waited for; matrix products, arithmetic and copies ran while one was open for 0% of the time, Pallas kernels for 9%

profile of v3, /device:TPU:14, one launch (start us, length us, event | category | flops | bytes accessed | tf_op | source)
XLA Modules:
  0.0 71.8 jit_solution(5791685071298858740)
XLA Ops:
  0.0 2.5 %project.1 = (bf16[136,128]{1,0:T(8,128)(2,1)}, bf16[136,128]{1,0:T(8,128)(2,1)}) custom-call(bf16[16,32,256]{2,1,0:T(8,128)(2,1)} %refs_0_.1, s32[16,32]{1,0:T(8,128)} %refs_1_.1, s32[1,32]{1,0:T(1,128)} %bitcast.24, f32[1,256]{1,0:T(1,128)} %bitcast.22, f32[1,256]{1,0:T(1,128)} %bitcast.23, bf16[64,256]{1,0:T(8,128)(2,1)} %bitcast.21, f32[1,64]{1,0:T(1,128)} %bitcast.25), custom_call_target="tpu_custom_call" | custom-call | flops 40000000 | bytes 524288 | tf_op jit(solution)/shard_map/project/pallas_call | solution.py:84
  2.5 12.5 %collective-permute-start = (bf16[136,128]{1,0:T(8,128)(2,1)}, bf16[136,128]{1,0:T(8,128)(2,1)S(1)}, u32[]{:S(2)}, u32[]{:S(2)}) collective-permute-start(bf16[136,128]{1,0:T(8,128)(2,1)} %get-tuple-element.13), channel_id=1, source_target_pairs={{0,0},{1,32},{2,64},{3,96},{4,128},{5,160},{6,192},{7,224},{8,256}... | collective-permute-start | bytes 104456 | tf_op jit(solution)/shard_map/ppermute | solution.py:220
  15.0 2.1 %fan.1 = bf16[32,136,128]{2,1,0:T(8,128)(2,1)} custom-call(bf16[136,128]{1,0:T(8,128)(2,1)} %get-tuple-element.12.a_ref), custom_call_target="tpu_custom_call" | custom-call | flops 1000000000 | bytes 2097152 | tf_op jit(solution)/shard_map/fan/pallas_call | solution.py:109
  17.1 0.0 copy-start
  17.1 10.3 %all-to-all-start = ((bf16[32,136,128]{2,1,0:T(8,128)(2,1)}), bf16[32,136,128]{2,1,0:T(8,128)(2,1)}, u32[]{:S(2)}, u32[]{:S(2)}) async-start(bf16[32,136,128]{2,1,0:T(8,128)(2,1)} %fan.1), calls=%async_computation | async-start | bytes 2228224 | tf_op jit(solution)/shard_map/all_to_all | solution.py:222
  27.5 0.0 copy-done
  27.5 0.1 copy.12
  27.6 0.1 copy.13.w_ref
  27.8 0.0 collective-permute-done
  27.8 30.8 %all-gather = bf16[2176,128]{1,0:T(8,128)(2,1)S(1)} all-gather(bf16[136,128]{1,0:T(8,128)(2,1)S(1)} %collective-permute-done), channel_id=2, replica_groups=mesh['z'=16,'xl'=2,'y'=4,'xh'=2,'core'=2] {'z'}, dimensions={0}, use_global_device_ids=true | all-gather | bytes 591872 | tf_op jit(solution)/shard_map/all_gather | solution.py:223
  58.6 0.0 copy-start.1
  58.6 0.1 columns.1
  58.8 0.0 all-to-all-done
  58.8 0.5 copy-done.1
  59.3 0.1 broadcast_in_dim.22.bias_ref
  59.3 3.3 %foreign.1 = bf16[32,32,128]{2,1,0:T(8,128)(2,1)S(1)} custom-call(s32[1]{0:T(128)} %bitcast.xl_ref, bf16[2,16,136,128]{3,2,1,0:T(8,128)(2,1)} %bitcast.6.a_ref, bf16[256,1024]{1,0:T(8,128)(2,1)S(1)} %get-tuple-element.17.b_ref, bf16[128,128]{1,0:T(8,128)(2,1)S(1)} %get-tuple-element.18.wb_ref, bf16[512,256]{1,0:T(8,128)(2,1)S(1)} %copy.13.w_ref, ...), custom_call_target="tpu_custom_call" | custom-call | flops 1000000000 | bytes 2097152 | tf_op jit(solution)/shard_map/foreign/pallas_call | solution.py:200
  62.7 2.3 %collective-permute-start.1 = (bf16[32,32,128]{2,1,0:T(8,128)(2,1)S(1)}, bf16[32,32,128]{2,1,0:T(8,128)(2,1)S(1)}, u32[]{:S(2)}, u32[]{:S(2)}) collective-permute-start(bf16[32,32,128]{2,1,0:T(8,128)(2,1)S(1)} %foreign.1), channel_id=1, source_target_pairs={{0,16},{16,0},{1,17},{17,1},{2,18},{18,2},{3,19},{19,3},{4,20},{20... | collective-permute-start | bytes 786440 | tf_op jit(solution)/shard_map/ppermute | solution.py:234
  65.0 4.1 %own.1.given_ref = f32[32,64,128]{2,1,0:T(8,128)} custom-call(s32[1]{0:T(128)} %bitcast.xl_ref, bf16[2,16,136,128]{3,2,1,0:T(8,128)(2,1)} %bitcast.6.a_ref, bf16[256,1024]{1,0:T(8,128)(2,1)S(1)} %get-tuple-element.17.b_ref, bf16[128,128]{1,0:T(8,128)(2,1)S(1)} %get-tuple-element.18.wb_ref, bf16[512,256]{1,0:T(8,128)(2,1)S(1)} %copy.13.w_ref, ...), custom_call_target="tpu_custom_call" | custom-call | flops 1000000000 | bytes 2097152 | tf_op jit(solution)/shard_map/own/pallas_call | solution.py:200
  69.1 1.8 %collective-permute-done.1.t_ref = bf16[32,32,128]{2,1,0:T(8,128)(2,1)S(1)} collective-permute-done((bf16[32,32,128]{2,1,0:T(8,128)(2,1)S(1)}, bf16[32,32,128]{2,1,0:T(8,128)(2,1)S(1)}, u32[]{:S(2)}, u32[]{:S(2)}) %collective-permute-start.1) | collective-permute-done | bytes 262176 | tf_op jit(solution)/shard_map/ppermute | solution.py:234
  70.9 0.8 %join.1 = f32[32,64,128]{2,1,0:T(8,128)} custom-call(s32[1]{0:T(128)} %bitcast.xl_ref, bf16[32,32,128]{2,1,0:T(8,128)(2,1)S(1)} %collective-permute-done.1.t_ref, f32[32,64,128]{2,1,0:T(8,128)} %own.1.given_ref), custom_call_target="tpu_custom_call", output_to_operand_aliasing={{}: (2, {})} | custom-call | flops 1000000 | bytes 2097152 | tf_op jit(solution)/shard_map/join/pallas_call | solution.py:200
  (1 shorter events, 0.0 us)
Async XLA Ops:
  2.5 25.3 %collective-permute-start = (bf16[136,128]{1,0:T(8,128)(2,1)}, bf16[136,128]{1,0:T(8,128)(2,1)S(1)}, u32[]{:S(2)}, u32[]{:S(2)}) collective-permute-start(bf16[136,128]{1,0:T(8,128)(2,1)} %get-tuple-element.13), channel_id=1, source_target_pairs={{0,0},{1,32},{2,64},{3,96},{4,128},{5,160},{6,192},{7,224},{8,256}... | collective-permute-start | bytes 104456 | tf_op jit(solution)/shard_map/ppermute | solution.py:220
  17.1 10.3 %copy-start = (bf16[1024,128]{1,0:T(8,128)(2,1)S(1)}, bf16[1024,128]{1,0:T(8,128)(2,1)}, u32[]{:S(2)}) copy-start(bf16[1024,128]{1,0:T(8,128)(2,1)} %param.16) | copy-start | bytes 786436
  17.1 41.6 %all-to-all-start = ((bf16[32,136,128]{2,1,0:T(8,128)(2,1)}), bf16[32,136,128]{2,1,0:T(8,128)(2,1)}, u32[]{:S(2)}, u32[]{:S(2)}) async-start(bf16[32,136,128]{2,1,0:T(8,128)(2,1)} %fan.1), calls=%async_computation | async-start | bytes 2228224 | tf_op jit(solution)/shard_map/all_to_all | solution.py:222
  58.6 0.7 copy-start.1
  62.7 8.3 %collective-permute-start.1 = (bf16[32,32,128]{2,1,0:T(8,128)(2,1)S(1)}, bf16[32,32,128]{2,1,0:T(8,128)(2,1)S(1)}, u32[]{:S(2)}, u32[]{:S(2)}) collective-permute-start(bf16[32,32,128]{2,1,0:T(8,128)(2,1)S(1)} %foreign.1), channel_id=1, source_target_pairs={{0,16},{16,0},{1,17},{17,1},{2,18},{18,2},{3,19},{19,3},{4,20},{20... | collective-permute-start | bytes 786440 | tf_op jit(solution)/shard_map/ppermute | solution.py:234

commit v4 on v3

v4 whole, which is shorter than its diff:
```python
import jax
import jax.numpy as jnp
from jax import lax
from jax.experimental import pallas as pl
from jax.experimental.pallas import tpu as pltpu
from jax.sharding import Mesh, PartitionSpec as P

EPSILON = 1e-05
RES = ("z", "xl")
SEQ = ("y", "xh", "core")


def iota(shape, dim):
    return lax.broadcasted_iota(jnp.int32, shape, dim)


def ones_where(condition, dtype=jnp.bfloat16):
    return jnp.where(condition, 1.0, 0.0).astype(dtype)


def project_kernel(*refs):
    sources, (copies_ref, b_ref, tile_ref), held, (pa, tiles, a_ref, sems) = refs[:8], refs[8:11], refs[11:19], refs[19:]
    small = [pltpu.make_async_copy(src, dst, sems.at[k]) for k, (src, dst) in enumerate(zip(sources[1:], held[1:]))]
    large = pltpu.make_async_copy(sources[0], held[0], sems.at[7])
    for load in [large] + small:
        load.start()
    x_ref, mask_ref, present_ref, gain_ref, bias_ref, w_ref, pb_ref, ob_ref = held
    for load in small:
        load.wait()
    weights = (mask_ref[...] * present_ref[...]).astype(jnp.float32).astype(jnp.bfloat16)
    proj_w = w_ref[...]

    row, col = iota((32, 64), 0), iota((32, 64), 1)
    pick = ones_where(col == 32 + 4 * (row % 8) + row // 8)
    wb = jnp.dot(pick, proj_w, preferred_element_type=jnp.float32).astype(jnp.bfloat16)
    row, col = iota((8, 64), 0), iota((8, 64), 1)
    own = jnp.where((col >= 32) & ((col - 32) // 4 == row), pb_ref[...], 0.0)
    row, lane = iota((64, 128), 0), iota((64, 128), 1) // 32
    spread = ones_where(row % 4 == lane, jnp.float32)
    b_bias = jnp.dot(own, spread, precision=lax.Precision.HIGHEST, preferred_element_type=jnp.float32)
    four = ones_where(row == iota((64, 128), 1) % 32)
    wa = lax.dot_general(four, proj_w, (((0,), (0,)), ((), ())), preferred_element_type=jnp.float32)
    wa = wa.astype(jnp.bfloat16)
    a_bias = jnp.dot(jnp.broadcast_to(pb_ref[...], (8, 64)), four.astype(jnp.float32),
                     precision=lax.Precision.HIGHEST, preferred_element_type=jnp.float32)
    tile_ref[...] = jnp.broadcast_to(ob_ref[...], (128, 128)).T

    large.wait()
    value = x_ref[...].reshape(512, 256).astype(jnp.float32)
    mean = jnp.mean(value, axis=-1, keepdims=True)
    centred = value - mean
    var = jnp.mean(centred * centred, axis=-1, keepdims=True)
    normed = (centred * lax.rsqrt(var + EPSILON) * gain_ref[...] + bias_ref[...]).astype(jnp.bfloat16)
    pa[...] = lax.dot_general(normed, wa, (((1,), (1,)), ((), ())), preferred_element_type=jnp.float32) + a_bias[0:1]
    row, lane128 = iota((32, 128), 0), iota((32, 128), 1)
    group = iota((16, 128), 1) // 32
    for g in range(8):
        part = [pa[pl.ds(4 * g + k, 16, stride=32), :] for k in range(4)]
        out = jnp.where(group < 2, jnp.where(group == 0, part[0], part[1]), jnp.where(group == 2, part[2], part[3]))
        spread = jnp.dot(weights, ones_where(row == 4 * g + lane128 // 32), preferred_element_type=jnp.float32)
        a_ref[0, g * 16:(g + 1) * 16, :] = (out * spread).astype(jnp.bfloat16)
    a_plain = jnp.dot(weights, ones_where(lane128 == (row % 4) * 8 + row // 4), preferred_element_type=jnp.float32)
    a_ref[0, 128:136, :] = (a_plain[:8] + pltpu.roll(a_plain[8:], 64, 1)).astype(jnp.bfloat16)
    for k in range(1, 4):
        a_ref[k] = a_ref[0]
    copies = [pltpu.make_async_copy(a_ref, copies_ref.at[pl.ds(4 * k, 4)], sems.at[8 + k]) for k in range(8)]
    for copy in copies:
        copy.start()

    bt = lax.dot_general(wb, normed, (((1,), (1,)), ((), ())), preferred_element_type=jnp.float32)
    group = iota((8, 128), 1) // 32
    for t in range(4):
        parts = [bt[p * 8:(p + 1) * 8, t * 128:(t + 1) * 128] for p in range(4)]
        for r in range(4):
            out = parts[r]
            for p in range(4):
                if p != r:
                    out = jnp.where(group == p, pltpu.roll(parts[p], (32 * (p - r)) % 128, 1), out)
            tiles[pl.ds(4 * t + r, 8, stride=16), :] = out + b_bias
    b_weights = jnp.dot(weights, ones_where(lane128 % 32 == row), preferred_element_type=jnp.float32)
    for g in range(8):
        b_ref[g * 16:(g + 1) * 16, :] = (tiles[g * 16:(g + 1) * 16, :] * b_weights).astype(jnp.bfloat16)
    b_plain = jnp.where(iota((16, 128), 1) < 32, b_weights, 0.0)
    b_ref[128:136, :] = (b_plain[:8] + pltpu.roll(b_plain[8:], 64, 1)).astype(jnp.bfloat16)
    for copy in copies:
        copy.wait()


def project(x, mask, present, gain, bias, weight, proj_bias, out_bias):
    vmem = pl.BlockSpec(memory_space=pltpu.VMEM)
    out = [jax.ShapeDtypeStruct((32, 136, 128), jnp.bfloat16), jax.ShapeDtypeStruct((136, 128), jnp.bfloat16),
           jax.ShapeDtypeStruct((128, 128), jnp.float32)]
    given = (x, mask, present[None], gain[None], bias[None], weight.T, proj_bias[None], out_bias[None])
    return pl.pallas_call(
        project_kernel,
        out_shape=out,
        in_specs=[pl.BlockSpec(memory_space=pl.ANY)] * 8,
        out_specs=[pl.BlockSpec(memory_space=pl.ANY), vmem, vmem],
        scratch_shapes=[pltpu.VMEM(g.shape, g.dtype) for g in given] + [
            pltpu.VMEM((512, 128), jnp.float32), pltpu.VMEM((128, 128), jnp.float32),
            pltpu.VMEM((4, 136, 128), jnp.bfloat16), pltpu.SemaphoreType.DMA((16,))],
        compiler_params=pltpu.CompilerParams(vmem_limit_bytes=56 * 1024 * 1024),
        cost_estimate=pl.CostEstimate(flops=4 * 10**7, bytes_accessed=2**19, transcendentals=0),
        name="project",
    )(*given)


OFFSETS = ((2, 1), (1, 1), (3, 1), (2, 0), (0, 1), (1, 0), (3, 0), (0, 0))
PACKED = sum((y * 2 + xh) << 3 * k for k, (y, xh) in enumerate(OFFSETS))


def source(line, z):
    dz = (z - line) & 15
    rank = 2 * jnp.minimum(dz, 16 - dz) - jnp.where((dz >= 1) & (dz <= 8), 1, 0)
    offset = (PACKED >> (3 * (rank >> 1))) & 7
    y = (line >> 2) + (offset >> 1)
    xh = (line >> 1) ^ offset
    return (y & 3) * 4 + (xh & 1) * 2 + (rank & 1)


def columns_kernel(line_ref, b_ref, tile_ref, o_ref, wb_ref, bias_ref, packed):
    for z in range(16):
        at = source(line_ref[0], jnp.int32(z))
        rows = pl.ds(pl.multiple_of(at * 16, 16), 16)
        for g in range(8):
            v = b_ref[z, g * 16:(g + 1) * 16, :]
            o_ref[0, rows, g * 128:(g + 1) * 128] = v
            o_ref[1, rows, g * 128:(g + 1) * 128] = pltpu.roll(v.astype(jnp.float32), 64, 1).astype(jnp.bfloat16)
        packed[pl.ds(pl.multiple_of(at * 8, 8), 8), :] = b_ref[z, 128:136, :].astype(jnp.float32)
    wb_ref[...] = packed[...].astype(jnp.bfloat16)
    bias_ref[...] = tile_ref[...]


def columns(line, b_all, bias):
    vmem = pl.BlockSpec(memory_space=pltpu.VMEM)
    return pl.pallas_call(
        columns_kernel,
        out_shape=[jax.ShapeDtypeStruct((2, 256, 1024), jnp.bfloat16), jax.ShapeDtypeStruct((128, 128), jnp.bfloat16),
                   jax.ShapeDtypeStruct((128, 128), jnp.float32)],
        in_specs=[pl.BlockSpec(memory_space=pltpu.SMEM), vmem, vmem],
        out_specs=[vmem] * 3,
        scratch_shapes=[pltpu.VMEM((128, 128), jnp.float32)],
        compiler_params=pltpu.CompilerParams(vmem_limit_bytes=16 * 1024 * 1024),
        cost_estimate=pl.CostEstimate(flops=3*10**10, bytes_accessed=2**21, transcendentals=0),
        name="columns",
    )(line, b_all, bias)


def tile(block, a_ref, b_ref, wb_ref, w_ref, bias_ref, at, xs, put):
    lane = iota((128, 128), 1)
    for g in range(8):
        t = a_ref[block, :, g * 16:(g + 1) * 16, :].reshape(256, 128).T
        for k in range(4):
            i = 4 * g + k
            row = (i % 2) * 512 + (i // 2) * 32
            at[row:row + 32, :] = t[k * 32:(k + 1) * 32, :]
    wa = a_ref[block, :, 128:136, :].astype(jnp.float32).reshape(128, 128).astype(jnp.bfloat16)
    count = lax.dot_general(wa, wb_ref[...], (((0,), (0,)), ((), ())), preferred_element_type=jnp.float32)
    count = jnp.where(lane[:32] < 32, count[0:32] + pltpu.roll(count[64:96], 64, 1), 0.0)
    spread = count[0:8]
    for k in range(1, 4):
        spread += pltpu.roll(count[k * 8:(k + 1) * 8], 32 * (0, 2, 1, 3)[k], 1)
    inv = 1.0 / jnp.maximum(spread, 1.0)
    bias = bias_ref[...]
    low = lane < 64
    even = (lane // 32) % 2 == 0
    for n in range(4):
        for m in range(2):
            o = [jnp.dot(at[h * 512 + m * 256:h * 512 + (m + 1) * 256, :], b_ref[h, :, n * 256:(n + 1) * 256],
                         preferred_element_type=jnp.float32) for h in range(2)]
            for k in range(8):
                pair = m * 8 + k
                for t in range(2):
                    g = 2 * n + t
                    o0, o1 = (v[k * 32:(k + 1) * 32, t * 128:(t + 1) * 128] for v in o)
                    at_lane = slice((pair % 2) * 128, (pair % 2 + 1) * 128)
                    xs[0, pair // 2, g * 32:(g + 1) * 32, at_lane] = jnp.where(low[:32], o0, o1).astype(jnp.bfloat16)
                    xs[1, pair // 2, g * 32:(g + 1) * 32, at_lane] = jnp.where(low[:32], o1, o0).astype(jnp.bfloat16)
    for q in range(8):
        y = [jnp.dot(w_ref[h * 256:(h + 1) * 256, :], xs[h, q], preferred_element_type=jnp.float32) for h in range(2)]
        z = []
        for k in range(2):
            s0, s1 = (jnp.where(even, v[:128, k * 128:(k + 1) * 128], v[128:, k * 128:(k + 1) * 128]) for v in y)
            r = s0 + pltpu.roll(s1, 64, 1)
            z.append(r + pltpu.roll(r, 32 if k else 96, 1))
        put(q, ((jnp.where(even, z[0], z[1]) + bias) * inv[q:q + 1]).T)


def foreign_kernel(xl_ref, a_ref, b_ref, wb_ref, w_ref, bias_ref, o_ref, at, xs):
    def put(q, z):
        for k in range(4):
            o_ref[4 * q + (0, 2, 1, 3)[k]] = z[k * 32:(k + 1) * 32].astype(jnp.bfloat16)

    tile(1 - xl_ref[0], a_ref, b_ref, wb_ref, w_ref, bias_ref, at, xs, put)


def own_kernel(xl_ref, a_ref, b_ref, wb_ref, w_ref, bias_ref, o_ref, at, xs, held, sems):
    place = pl.ds(pl.multiple_of(xl_ref[0] * 32, 32), 32)
    copies = [pltpu.make_async_copy(held.at[pl.ds(4 * q, 4)], o_ref.at[pl.ds(4 * q, 4), place, :], sems.at[q])
              for q in range(8)]

    def put(q, z):
        for k in range(4):
            held[4 * q + (0, 2, 1, 3)[k]] = z[k * 32:(k + 1) * 32]
        copies[q].start()

    tile(xl_ref[0], a_ref, b_ref, wb_ref, w_ref, bias_ref, at, xs, put)
    for copy in copies:
        copy.wait()


def join_kernel(xl_ref, t_ref, given_ref, o_ref, held, sems):
    del given_ref
    place = pl.ds(pl.multiple_of((1 - xl_ref[0]) * 32, 32), 32)
    copies = [pltpu.make_async_copy(held.at[pl.ds(4 * q, 4)], o_ref.at[pl.ds(4 * q, 4), place, :], sems.at[q])
              for q in range(8)]
    for q in range(8):
        held[4 * q:4 * q + 4] = t_ref[4 * q:4 * q + 4].astype(jnp.float32)
        copies[q].start()
    for copy in copies:
        copy.wait()


def call(kernel, name, shape, dtype, out_space, scratch, flops, in_specs, aliases, args):
    return pl.pallas_call(
        kernel,
        out_shape=jax.ShapeDtypeStruct(shape, dtype),
        in_specs=in_specs,
        out_specs=pl.BlockSpec(memory_space=out_space),
        scratch_shapes=scratch,
        input_output_aliases=aliases,
        compiler_params=pltpu.CompilerParams(vmem_limit_bytes=24 * 1024 * 1024),
        cost_estimate=pl.CostEstimate(flops=flops, bytes_accessed=2**21, transcendentals=0),
        name=name,
    )(*args)


def shift(n, by):
    return [(i, (i + by) % n) for i in range(n)]


def places():
    out = []
    for line in range(16):
        row = []
        for z in range(16):
            dz = (z - line) % 16
            rank = 2 * min(dz, 16 - dz) - int(1 <= dz <= 8)
            y, xh = OFFSETS[rank // 2]
            row.append((line // 4 + y) % 4 * 4 + (line // 2 % 2 ^ xh) * 2 + rank % 2)
        out.append(row)
    return out


def local(x, mask, present, gain, bias, weight, proj_bias, out_weight, out_bias):
    a, b, bias2 = project(x, mask, present, gain, bias, weight, proj_bias, out_bias)
    turn = [((z * 2 + xl) * 16 + q, (at * 2 + xl) * 16 + z) for z, row in enumerate(places()) for xl in range(2)
            for at, q in enumerate(row)]
    b = lax.ppermute(b, RES + SEQ, turn)
    w4 = out_weight.reshape(32, 8, 4, 128).transpose(2, 3, 1, 0).reshape(512, 256)
    a_all = lax.all_to_all(a, ("xl",) + SEQ, 0, 0, tiled=True).reshape(2, 16, 136, 128)
    b_all = lax.all_gather(b, "z")
    line = sum(lax.axis_index(n) * k for n, k in zip(SEQ, (4, 2, 1))).astype(jnp.int32).reshape(1)
    b_all, wb, bias2 = columns(line, b_all, bias2)
    a_all, b_all = lax.optimization_barrier((a_all, b_all))

    xl = lax.axis_index("xl").astype(jnp.int32).reshape(1)
    smem, vmem, anywhere = (pl.BlockSpec(memory_space=m) for m in (pltpu.SMEM, pltpu.VMEM, pl.ANY))
    work = [pltpu.VMEM((1024, 256), jnp.bfloat16), pltpu.VMEM((2, 8, 256, 256), jnp.bfloat16)]
    held = [pltpu.VMEM((32, 32, 128), jnp.float32), pltpu.SemaphoreType.DMA((8,))]
    args, specs = (xl, a_all, b_all, wb, w4, bias2), [smem] + [vmem] * 5
    sent = call(foreign_kernel, "foreign", (32, 32, 128), jnp.bfloat16, pltpu.VMEM, work, 10**9, specs, {}, args)
    taken = lax.ppermute(sent, "xl", shift(2, 1))
    out = call(own_kernel, "own", (32, 64, 128), jnp.float32, pl.ANY, work + held, 10**9, specs, {}, args)
    return call(join_kernel, "join", (32, 64, 128), jnp.float32, pl.ANY, held, 10**6, [smem, vmem, anywhere], {2: 0},
                (xl, taken, out))


def solution(mesh):
    fine = Mesh(mesh.devices.reshape(16, 2, 4, 2, 2), RES + SEQ)
    in_specs = (P(SEQ, RES, None), P(SEQ, RES), P(RES), P(), P(), P(), P(), P(), P())
    return jax.shard_map(local, mesh=fine, in_specs=in_specs, out_specs=P(RES, SEQ, None), check_vma=False)
```

time: 72.2 us -> 68.2 us (0.945)
  Pallas kernels: 13 us -> 9.09 us
  starting transfers between devices: 25.2 us -> 23 us
  blocking collectives: 30.8 us -> 32.4 us
  waiting for transfers between devices: 1.84 us -> 3.12 us
    pallas_call x3, Pallas kernels: 8.25 us -> 5.31 us  [call(): pl.pallas_call(kernel, out_shape=jax.ShapeDtypeStruct(shape, dtype), in_s...]
    all_to_all x1, starting transfers between devices: 10.3 us -> 8.27 us  [local(): lax.all_to_all(a, ('xl',) + SEQ, 0, 0, tiled=True).reshape(2, 16, 136, 128)]
    pallas_call x2 -> x1, Pallas kernels: 2.22 us -> 0.24 us  [columns(): pl.pallas_call(columns_kernel, out_shape=[jax.ShapeDtypeStruct((2, 256, 1...]
    all_gather x1, blocking collectives: 30.8 us -> 32.4 us  [local(): b_all = lax.all_gather(b, 'z')]
    ppermute x1, waiting for transfers between devices: 1.84 us -> 3.11 us  [local(): taken = lax.ppermute(sent, 'xl', shift(2, 1))]
    pallas_call x1, Pallas kernels: 2.5 us -> 3.54 us  [project(): pl.pallas_call(project_kernel, out_shape=out, in_specs=[pl.BlockSpec(memo...]
  transfers between devices with their start and end apart: 3 -> 3, of which waited for: 1 -> 1; matrix products, arithmetic and copies ran while one was open for 0% -> 0% of each run, Pallas kernels for 9% -> 4%
where the time goes in v4:
time: 68.2 us; the launch traced here: 68 us
  blocking collectives  32.4 us (48%)
  starting transfers between devices  23 us (34%)
  Pallas kernels  9.09 us (13%)
  waiting for transfers between devices  3.12 us (5%)
    all_gather x1, blocking collectives, local(): b_all = lax.all_gather(b, 'z')  32.4 us
    ppermute x1, starting transfers between devices, local(): b = lax.ppermute(b, RES + SEQ, turn)  12.1 us
    all_to_all x1, starting transfers between devices, local(): lax.all_to_all(a, ('xl',) + SEQ, 0, 0, tiled=True).reshape(2, 16, 136, 128)  8.27 us
    pallas_call x3, Pallas kernels, call(): pl.pallas_call(kernel, out_shape=jax.ShapeDtypeStruct(shape, dtype), in_s...  5.31 us
    pallas_call x1, Pallas kernels, project(): pl.pallas_call(project_kernel, out_shape=out, in_specs=[pl.BlockSpec(memo...  3.54 us
    ppermute x1, waiting for transfers between devices, local(): taken = lax.ppermute(sent, 'xl', shift(2, 1))  3.11 us
    ppermute x1, starting transfers between devices, local(): taken = lax.ppermute(sent, 'xl', shift(2, 1))  2.56 us
  transfers between devices with their start and end apart: 3, of which 1 were waited for; matrix products, arithmetic and copies ran while one was open for 0% of the time, Pallas kernels for 4%

profile of v4, /device:TPU:14, one launch (start us, length us, event | category | flops | bytes accessed | tf_op | source)
XLA Modules:
  0.0 68.0 jit_solution(3713210019326896260)
XLA Ops:
  0.0 3.5 %project.1 = (bf16[32,136,128]{2,1,0:T(8,128)(2,1)}, bf16[136,128]{1,0:T(8,128)(2,1)}, f32[128,128]{1,0:T(8,128)}) custom-call(bf16[16,32,256]{2,1,0:T(8,128)(2,1)} %refs_0_.1, s32[16,32]{1,0:T(8,128)} %refs_1_.1, s32[1,32]{1,0:T(1,128)} %bitcast.28, f32[1,256]{1,0:T(1,128)} %bitcast.26, f32[1,256]{1,0:T(1,128)} %bitcast.27, bf16[64,256]{1,0:T(8,128)(2,1)} %bitcast.25, ...), custom_call_target="tpu_custom_call" | custom-call | flops 40000000 | bytes 524288 | tf_op jit(solution)/shard_map/project/pallas_call | solution.py:94
  3.5 12.1 %collective-permute-start = (bf16[136,128]{1,0:T(8,128)(2,1)}, bf16[136,128]{1,0:T(8,128)(2,1)S(1)}, u32[]{:S(2)}, u32[]{:S(2)}) collective-permute-start(bf16[136,128]{1,0:T(8,128)(2,1)} %get-tuple-element.14), channel_id=1, source_target_pairs={{10,0},{11,32},{7,64},{15,96},{9,128},{3,160},{5,192},{13,224},{1,... | collective-permute-start | bytes 104456 | tf_op jit(solution)/shard_map/ppermute | solution.py:259
  15.7 0.0 copy-start.1
  15.7 8.3 %all-to-all-start = ((bf16[32,136,128]{2,1,0:T(8,128)(2,1)}), bf16[32,136,128]{2,1,0:T(8,128)(2,1)S(1)}, u32[]{:S(2)}, u32[]{:S(2)}) async-start(bf16[32,136,128]{2,1,0:T(8,128)(2,1)} %get-tuple-element.13), calls=%async_computation | async-start | bytes 2228224 | tf_op jit(solution)/shard_map/all_to_all | solution.py:261
  24.0 0.0 copy-start
  24.0 0.0 copy-done.1
  24.0 0.1 copy.12
  24.2 0.1 copy.13.w_ref
  24.3 0.0 collective-permute-done
  24.3 32.4 %all-gather = bf16[2176,128]{1,0:T(8,128)(2,1)S(1)} all-gather(bf16[136,128]{1,0:T(8,128)(2,1)S(1)} %collective-permute-done), channel_id=2, replica_groups=mesh['z'=16,'xl'=2,'y'=4,'xh'=2,'core'=2] {'z'}, dimensions={0}, use_global_device_ids=true | all-gather | bytes 591872 | tf_op jit(solution)/shard_map/all_gather | solution.py:262
  56.7 0.0 copy-done
  56.7 0.2 columns.1
  56.9 0.0 all-to-all-done
  56.9 1.9 %foreign.1 = bf16[32,32,128]{2,1,0:T(8,128)(2,1)S(1)} custom-call(s32[1]{0:T(128)} %bitcast.xl_ref, bf16[2,16,136,128]{3,2,1,0:T(8,128)(2,1)S(1)} %bitcast.19, bf16[2,256,1024]{2,1,0:T(8,128)(2,1)S(1)} %get-tuple-element.18.b_ref, bf16[128,128]{1,0:T(8,128)(2,1)S(1)} %get-tuple-element.19.wb_ref, bf16[512,256]{1,0:T(8,128)(2,1)S(1)} %copy.13.w_ref, ...), custom_call_target="tpu_custom_call" | custom-call | flops 1000000000 | bytes 2097152 | tf_op jit(solution)/shard_map/foreign/pallas_call | solution.py:225
  58.8 2.6 %collective-permute-start.1 = (bf16[32,32,128]{2,1,0:T(8,128)(2,1)S(1)}, bf16[32,32,128]{2,1,0:T(8,128)(2,1)S(1)}, u32[]{:S(2)}, u32[]{:S(2)}) collective-permute-start(bf16[32,32,128]{2,1,0:T(8,128)(2,1)S(1)} %foreign.1), channel_id=1, source_target_pairs={{0,16},{16,0},{1,17},{17,1},{2,18},{18,2},{3,19},{19,3},{4,20},{20... | collective-permute-start | bytes 786440 | tf_op jit(solution)/shard_map/ppermute | solution.py:273
  61.4 2.6 %own.1.given_ref = f32[32,64,128]{2,1,0:T(8,128)} custom-call(s32[1]{0:T(128)} %bitcast.xl_ref, bf16[2,16,136,128]{3,2,1,0:T(8,128)(2,1)S(1)} %bitcast.20, bf16[2,256,1024]{2,1,0:T(8,128)(2,1)S(1)} %get-tuple-element.18.b_ref, bf16[128,128]{1,0:T(8,128)(2,1)S(1)} %get-tuple-element.19.wb_ref, bf16[512,256]{1,0:T(8,128)(2,1)S(1)} %copy.13.w_ref, ...), custom_call_target="tpu_custom_call" | custom-call | flops 1000000000 | bytes 2097152 | tf_op jit(solution)/shard_map/own/pallas_call | solution.py:225
  64.0 3.1 %collective-permute-done.1.t_ref = bf16[32,32,128]{2,1,0:T(8,128)(2,1)S(1)} collective-permute-done((bf16[32,32,128]{2,1,0:T(8,128)(2,1)S(1)}, bf16[32,32,128]{2,1,0:T(8,128)(2,1)S(1)}, u32[]{:S(2)}, u32[]{:S(2)}) %collective-permute-start.1) | collective-permute-done | bytes 262176 | tf_op jit(solution)/shard_map/ppermute | solution.py:273
  67.1 0.9 %join.1 = f32[32,64,128]{2,1,0:T(8,128)} custom-call(s32[1]{0:T(128)} %bitcast.xl_ref, bf16[32,32,128]{2,1,0:T(8,128)(2,1)S(1)} %collective-permute-done.1.t_ref, f32[32,64,128]{2,1,0:T(8,128)} %own.1.given_ref), custom_call_target="tpu_custom_call", output_to_operand_aliasing={{}: (2, {})} | custom-call | flops 1000000 | bytes 2097152 | tf_op jit(solution)/shard_map/join/pallas_call | solution.py:225
  (1 shorter events, 0.0 us)
Async XLA Ops:
  3.5 20.8 %collective-permute-start = (bf16[136,128]{1,0:T(8,128)(2,1)}, bf16[136,128]{1,0:T(8,128)(2,1)S(1)}, u32[]{:S(2)}, u32[]{:S(2)}) collective-permute-start(bf16[136,128]{1,0:T(8,128)(2,1)} %get-tuple-element.14), channel_id=1, source_target_pairs={{10,0},{11,32},{7,64},{15,96},{9,128},{3,160},{5,192},{13,224},{1,... | collective-permute-start | bytes 104456 | tf_op jit(solution)/shard_map/ppermute | solution.py:259
  15.7 8.3 %copy-start.1 = (bf16[1024,128]{1,0:T(8,128)(2,1)S(1)}, bf16[1024,128]{1,0:T(8,128)(2,1)}, u32[]{:S(2)}) copy-start(bf16[1024,128]{1,0:T(8,128)(2,1)} %param.16) | copy-start | bytes 786436
  15.7 41.2 %all-to-all-start = ((bf16[32,136,128]{2,1,0:T(8,128)(2,1)}), bf16[32,136,128]{2,1,0:T(8,128)(2,1)S(1)}, u32[]{:S(2)}, u32[]{:S(2)}) async-start(bf16[32,136,128]{2,1,0:T(8,128)(2,1)} %get-tuple-element.13), calls=%async_computation | async-start | bytes 2228224 | tf_op jit(solution)/shard_map/all_to_all | solution.py:261
  24.0 32.7 %copy-start = (f32[128,128]{1,0:T(8,128)S(1)}, f32[128,128]{1,0:T(8,128)}, u32[]{:S(2)}) copy-start(f32[128,128]{1,0:T(8,128)} %get-tuple-element.15.tile_ref) | copy-start | bytes 196612
  58.8 8.3 %collective-permute-start.1 = (bf16[32,32,128]{2,1,0:T(8,128)(2,1)S(1)}, bf16[32,32,128]{2,1,0:T(8,128)(2,1)S(1)}, u32[]{:S(2)}, u32[]{:S(2)}) collective-permute-start(bf16[32,32,128]{2,1,0:T(8,128)(2,1)S(1)} %foreign.1), channel_id=1, source_target_pairs={{0,16},{16,0},{1,17},{17,1},{2,18},{18,2},{3,19},{19,3},{4,20},{20... | collective-permute-start | bytes 786440 | tf_op jit(solution)/shard_map/ppermute | solution.py:273

commit v5 on v4

--- a/solution.py
+++ b/solution.py
@@ -19,14 +19,16 @@
 
 
 def project_kernel(*refs):
-    sources, (copies_ref, b_ref, tile_ref), held, (pa, tiles, a_ref, sems) = refs[:8], refs[8:11], refs[11:19], refs[19:]
-    small = [pltpu.make_async_copy(src, dst, sems.at[k]) for k, (src, dst) in enumerate(zip(sources[1:], held[1:]))]
+    sources, (copies_ref, b_ref, tile_ref, w4_ref), held, (pa, tiles, a_ref, wf, sems) = refs[:9], refs[9:13], refs[13:22], refs[22:]
+    small = [pltpu.make_async_copy(src, dst, sems.at[k]) for k, (src, dst) in enumerate(zip(sources[1:8], held[1:8]))]
+    last = pltpu.make_async_copy(sources[8], held[8], sems.at[16])
     large = pltpu.make_async_copy(sources[0], held[0], sems.at[7])
-    for load in [large] + small:
+    for load in [large] + small + [last]:
         load.start()
-    x_ref, mask_ref, present_ref, gain_ref, bias_ref, w_ref, pb_ref, ob_ref = held
+    x_ref, mask_ref, present_ref, gain_ref, bias_ref, w_ref, pb_ref, ob_ref, ow_ref = held
     for load in small:
         load.wait()
+    large.wait()
     weights = (mask_ref[...] * present_ref[...]).astype(jnp.float32).astype(jnp.bfloat16)
     proj_w = w_ref[...]
 
@@ -45,7 +47,6 @@
                      precision=lax.Precision.HIGHEST, preferred_element_type=jnp.float32)
     tile_ref[...] = jnp.broadcast_to(ob_ref[...], (128, 128)).T
 
-    large.wait()
     value = x_ref[...].reshape(512, 256).astype(jnp.float32)
     mean = jnp.mean(value, axis=-1, keepdims=True)
     centred = value - mean
@@ -82,23 +83,28 @@
         b_ref[g * 16:(g + 1) * 16, :] = (tiles[g * 16:(g + 1) * 16, :] * b_weights).astype(jnp.bfloat16)
     b_plain = jnp.where(iota((16, 128), 1) < 32, b_weights, 0.0)
     b_ref[128:136, :] = (b_plain[:8] + pltpu.roll(b_plain[8:], 64, 1)).astype(jnp.bfloat16)
+    last.wait()
+    wf[...] = ow_ref[...].astype(jnp.float32)
+    for p in range(4):
+        rows = jnp.concatenate([wf[pl.ds(4 * g + p, 32, stride=32), :] for g in range(8)], axis=0)
+        w4_ref[p * 128:(p + 1) * 128, :] = rows.T.astype(jnp.bfloat16)
     for copy in copies:
         copy.wait()
 
 
-def project(x, mask, present, gain, bias, weight, proj_bias, out_bias):
+def project(x, mask, present, gain, bias, weight, proj_bias, out_bias, out_weight):
     vmem = pl.BlockSpec(memory_space=pltpu.VMEM)
     out = [jax.ShapeDtypeStruct((32, 136, 128), jnp.bfloat16), jax.ShapeDtypeStruct((136, 128), jnp.bfloat16),
-           jax.ShapeDtypeStruct((128, 128), jnp.float32)]
-    given = (x, mask, present[None], gain[None], bias[None], weight.T, proj_bias[None], out_bias[None])
+           jax.ShapeDtypeStruct((128, 128), jnp.float32), jax.ShapeDtypeStruct((512, 256), jnp.bfloat16)]
+    given = (x, mask, present[None], gain[None], bias[None], weight.T, proj_bias[None], out_bias[None], out_weight)
     return pl.pallas_call(
         project_kernel,
         out_shape=out,
-        in_specs=[pl.BlockSpec(memory_space=pl.ANY)] * 8,
-        out_specs=[pl.BlockSpec(memory_space=pl.ANY), vmem, vmem],
+        in_specs=[pl.BlockSpec(memory_space=pl.ANY)] * 9,
+        out_specs=[pl.BlockSpec(memory_space=pl.ANY), vmem, vmem, vmem],
         scratch_shapes=[pltpu.VMEM(g.shape, g.dtype) for g in given] + [
             pltpu.VMEM((512, 128), jnp.float32), pltpu.VMEM((128, 128), jnp.float32),
-            pltpu.VMEM((4, 136, 128), jnp.bfloat16), pltpu.SemaphoreType.DMA((16,))],
+            pltpu.VMEM((4, 136, 128), jnp.bfloat16), pltpu.VMEM((1024, 128), jnp.float32), pltpu.SemaphoreType.DMA((17,))],
         compiler_params=pltpu.CompilerParams(vmem_limit_bytes=56 * 1024 * 1024),
         cost_estimate=pl.CostEstimate(flops=4 * 10**7, bytes_accessed=2**19, transcendentals=0),
         name="project",
@@ -118,7 +124,7 @@
     return (y & 3) * 4 + (xh & 1) * 2 + (rank & 1)
 
 
-def columns_kernel(line_ref, b_ref, tile_ref, o_ref, wb_ref, bias_ref, packed):
+def columns_kernel(line_ref, b_ref, tile_ref, w_ref, o_ref, wb_ref, bias_ref, w4_ref, packed):
     for z in range(16):
         at = source(line_ref[0], jnp.int32(z))
         rows = pl.ds(pl.multiple_of(at * 16, 16), 16)
@@ -129,21 +135,22 @@
         packed[pl.ds(pl.multiple_of(at * 8, 8), 8), :] = b_ref[z, 128:136, :].astype(jnp.float32)
     wb_ref[...] = packed[...].astype(jnp.bfloat16)
     bias_ref[...] = tile_ref[...]
-
-
-def columns(line, b_all, bias):
+    w4_ref[...] = w_ref[...]
+
+
+def columns(line, b_all, bias, w4):
     vmem = pl.BlockSpec(memory_space=pltpu.VMEM)
     return pl.pallas_call(
         columns_kernel,
         out_shape=[jax.ShapeDtypeStruct((2, 256, 1024), jnp.bfloat16), jax.ShapeDtypeStruct((128, 128), jnp.bfloat16),
-                   jax.ShapeDtypeStruct((128, 128), jnp.float32)],
-        in_specs=[pl.BlockSpec(memory_space=pltpu.SMEM), vmem, vmem],
-        out_specs=[vmem] * 3,
+                   jax.ShapeDtypeStruct((128, 128), jnp.float32), jax.ShapeDtypeStruct((512, 256), jnp.bfloat16)],
+        in_specs=[pl.BlockSpec(memory_space=pltpu.SMEM), vmem, vmem, vmem],
+        out_specs=[vmem] * 4,
         scratch_shapes=[pltpu.VMEM((128, 128), jnp.float32)],
         compiler_params=pltpu.CompilerParams(vmem_limit_bytes=16 * 1024 * 1024),
         cost_estimate=pl.CostEstimate(flops=3*10**10, bytes_accessed=2**21, transcendentals=0),
         name="columns",
-    )(line, b_all, bias)
+    )(line, b_all, bias, w4)
 
 
 def tile(block, a_ref, b_ref, wb_ref, w_ref, bias_ref, at, xs, put):
@@ -253,15 +260,14 @@
 
 
 def local(x, mask, present, gain, bias, weight, proj_bias, out_weight, out_bias):
-    a, b, bias2 = project(x, mask, present, gain, bias, weight, proj_bias, out_bias)
+    a, b, bias2, w4 = project(x, mask, present, gain, bias, weight, proj_bias, out_bias, out_weight)
     turn = [((z * 2 + xl) * 16 + q, (at * 2 + xl) * 16 + z) for z, row in enumerate(places()) for xl in range(2)
             for at, q in enumerate(row)]
     b = lax.ppermute(b, RES + SEQ, turn)
-    w4 = out_weight.reshape(32, 8, 4, 128).transpose(2, 3, 1, 0).reshape(512, 256)
     a_all = lax.all_to_all(a, ("xl",) + SEQ, 0, 0, tiled=True).reshape(2, 16, 136, 128)
     b_all = lax.all_gather(b, "z")
     line = sum(lax.axis_index(n) * k for n, k in zip(SEQ, (4, 2, 1))).astype(jnp.int32).reshape(1)
-    b_all, wb, bias2 = columns(line, b_all, bias2)
+    b_all, wb, bias2, w4 = columns(line, b_all, bias2, w4)
     a_all, b_all = lax.optimization_barrier((a_all, b_all))
 
     xl = lax.axis_index("xl").astype(jnp.int32).reshape(1)

time: 68.2 us -> 67.9 us (level)
  the two profiles are of different devices: /device:TPU:14 before, /device:TPU:12 now
where the time goes in v5:
time: 67.9 us; the launch traced here: 67.6 us
  blocking collectives  32.4 us (48%)
  starting transfers between devices  23.3 us (34%)
  Pallas kernels  9.03 us (13%)
  waiting for transfers between devices  2.82 us (4%)
    all_gather x1, blocking collectives, local(): b_all = lax.all_gather(b, 'z')  32.4 us
    ppermute x1, starting transfers between devices, local(): b = lax.ppermute(b, RES + SEQ, turn)  11.2 us
    all_to_all x1, starting transfers between devices, local(): lax.all_to_all(a, ('xl',) + SEQ, 0, 0, tiled=True).reshape(2, 16, 136, 128)  9.17 us
    pallas_call x3, Pallas kernels, call(): pl.pallas_call(kernel, out_shape=jax.ShapeDtypeStruct(shape, dtype), in_s...  5.31 us
    pallas_call x1, Pallas kernels, project(): pl.pallas_call(project_kernel, out_shape=out, in_specs=[pl.BlockSpec(memo...  3.47 us
    ppermute x1, starting transfers between devices, local(): taken = lax.ppermute(sent, 'xl', shift(2, 1))  2.85 us
    ppermute x1, waiting for transfers between devices, local(): taken = lax.ppermute(sent, 'xl', shift(2, 1))  2.82 us
  transfers between devices with their start and end apart: 3, of which 1 were waited for; matrix products, arithmetic and copies ran while one was open for 0% of the time, Pallas kernels for 4%

profile of v5, /device:TPU:12, one launch (start us, length us, event | category | flops | bytes accessed | tf_op | source)
XLA Modules:
  0.0 67.6 jit_solution(9637763844072065324)
XLA Ops:
  0.0 3.5 %project.1 = (bf16[32,136,128]{2,1,0:T(8,128)(2,1)}, bf16[136,128]{1,0:T(8,128)(2,1)}, f32[128,128]{1,0:T(8,128)}, bf16[512,256]{1,0:T(8,128)(2,1)}) custom-call(bf16[16,32,256]{2,1,0:T(8,128)(2,1)} %refs_0_.1, s32[16,32]{1,0:T(8,128)} %refs_1_.1, s32[1,32]{1,0:T(1,128)} %bitcast.16, f32[1,256]{1,0:T(1,128)} %bitcast.14, f32[1,256]{1,0:T(1,128)} %bitcast.15, ...), custom_call_target="tpu_custom_call" | custom-call | flops 40000000 | bytes 524288 | tf_op jit(solution)/shard_map/project/pallas_call | solution.py:100
  3.5 11.2 %collective-permute-start = (bf16[136,128]{1,0:T(8,128)(2,1)}, bf16[136,128]{1,0:T(8,128)(2,1)S(1)}, u32[]{:S(2)}, u32[]{:S(2)}) collective-permute-start(bf16[136,128]{1,0:T(8,128)(2,1)} %get-tuple-element.16), channel_id=1, source_target_pairs={{10,0},{11,32},{7,64},{15,96},{9,128},{3,160},{5,192},{13,224},{1,... | collective-permute-start | bytes 104456 | tf_op jit(solution)/shard_map/ppermute | solution.py:266
  14.7 0.0 copy-start
  14.7 0.0 copy-start.1
  14.7 9.2 %all-to-all-start = ((bf16[32,136,128]{2,1,0:T(8,128)(2,1)}), bf16[32,136,128]{2,1,0:T(8,128)(2,1)S(1)}, u32[]{:S(2)}, u32[]{:S(2)}) async-start(bf16[32,136,128]{2,1,0:T(8,128)(2,1)} %get-tuple-element.15), calls=%async_computation | async-start | bytes 2228224 | tf_op jit(solution)/shard_map/all_to_all | solution.py:267
  23.9 0.0 collective-permute-done
  23.9 32.4 %all-gather = bf16[2176,128]{1,0:T(8,128)(2,1)S(1)} all-gather(bf16[136,128]{1,0:T(8,128)(2,1)S(1)} %collective-permute-done), channel_id=2, replica_groups=mesh['z'=16,'xl'=2,'y'=4,'xh'=2,'core'=2] {'z'}, dimensions={0}, use_global_device_ids=true | all-gather | bytes 591872 | tf_op jit(solution)/shard_map/all_gather | solution.py:268
  56.4 0.0 copy-done
  56.4 0.0 copy-done.1
  56.4 0.3 columns.1
  56.6 0.0 all-to-all-done
  56.6 1.9 %foreign.1 = bf16[32,32,128]{2,1,0:T(8,128)(2,1)S(1)} custom-call(s32[1]{0:T(128)} %bitcast.xl_ref, bf16[2,16,136,128]{3,2,1,0:T(8,128)(2,1)S(1)} %bitcast.10, bf16[2,256,1024]{2,1,0:T(8,128)(2,1)S(1)} %get-tuple-element.21.b_ref, bf16[128,128]{1,0:T(8,128)(2,1)S(1)} %get-tuple-element.22.wb_ref, bf16[512,256]{1,0:T(8,128)(2,1)S(1)} %get-tuple-element.23.w_ref, ...), custom_call_target="tpu_custom_call" | custom-call | flops 1000000000 | bytes 2097152 | tf_op jit(solution)/shard_map/foreign/pallas_call | solution.py:232
  58.5 2.8 %collective-permute-start.1 = (bf16[32,32,128]{2,1,0:T(8,128)(2,1)S(1)}, bf16[32,32,128]{2,1,0:T(8,128)(2,1)S(1)}, u32[]{:S(2)}, u32[]{:S(2)}) collective-permute-start(bf16[32,32,128]{2,1,0:T(8,128)(2,1)S(1)} %foreign.1), channel_id=1, source_target_pairs={{0,16},{16,0},{1,17},{17,1},{2,18},{18,2},{3,19},{19,3},{4,20},{20... | collective-permute-start | bytes 786440 | tf_op jit(solution)/shard_map/ppermute | solution.py:279
  61.4 2.6 %own.1.given_ref = f32[32,64,128]{2,1,0:T(8,128)} custom-call(s32[1]{0:T(128)} %bitcast.xl_ref, bf16[2,16,136,128]{3,2,1,0:T(8,128)(2,1)S(1)} %bitcast.11, bf16[2,256,1024]{2,1,0:T(8,128)(2,1)S(1)} %get-tuple-element.21.b_ref, bf16[128,128]{1,0:T(8,128)(2,1)S(1)} %get-tuple-element.22.wb_ref, bf16[512,256]{1,0:T(8,128)(2,1)S(1)} %get-tuple-element.23.w_ref, ...), custom_call_target="tpu_custom_call" | custom-call | flops 1000000000 | bytes 2097152 | tf_op jit(solution)/shard_map/own/pallas_call | solution.py:232
  64.0 2.8 %collective-permute-done.1.t_ref = bf16[32,32,128]{2,1,0:T(8,128)(2,1)S(1)} collective-permute-done((bf16[32,32,128]{2,1,0:T(8,128)(2,1)S(1)}, bf16[32,32,128]{2,1,0:T(8,128)(2,1)S(1)}, u32[]{:S(2)}, u32[]{:S(2)}) %collective-permute-start.1) | collective-permute-done | bytes 262176 | tf_op jit(solution)/shard_map/ppermute | solution.py:279
  66.8 0.9 %join.1 = f32[32,64,128]{2,1,0:T(8,128)} custom-call(s32[1]{0:T(128)} %bitcast.xl_ref, bf16[32,32,128]{2,1,0:T(8,128)(2,1)S(1)} %collective-permute-done.1.t_ref, f32[32,64,128]{2,1,0:T(8,128)} %own.1.given_ref), custom_call_target="tpu_custom_call", output_to_operand_aliasing={{}: (2, {})} | custom-call | flops 1000000 | bytes 2097152 | tf_op jit(solution)/shard_map/join/pallas_call | solution.py:232
Async XLA Ops:
  3.5 20.5 %collective-permute-start = (bf16[136,128]{1,0:T(8,128)(2,1)}, bf16[136,128]{1,0:T(8,128)(2,1)S(1)}, u32[]{:S(2)}, u32[]{:S(2)}) collective-permute-start(bf16[136,128]{1,0:T(8,128)(2,1)} %get-tuple-element.16), channel_id=1, source_target_pairs={{10,0},{11,32},{7,64},{15,96},{9,128},{3,160},{5,192},{13,224},{1,... | collective-permute-start | bytes 104456 | tf_op jit(solution)/shard_map/ppermute | solution.py:266
  14.7 41.6 %copy-start = (bf16[512,256]{1,0:T(8,128)(2,1)S(1)}, bf16[512,256]{1,0:T(8,128)(2,1)}, u32[]{:S(2)}) copy-start(bf16[512,256]{1,0:T(8,128)(2,1)} %get-tuple-element.18.w_ref) | copy-start | bytes 786436
  14.7 41.6 %copy-start.1 = (f32[128,128]{1,0:T(8,128)S(1)}, f32[128,128]{1,0:T(8,128)}, u32[]{:S(2)}) copy-start(f32[128,128]{1,0:T(8,128)} %get-tuple-element.17.tile_ref) | copy-start | bytes 196612
  14.7 41.9 %all-to-all-start = ((bf16[32,136,128]{2,1,0:T(8,128)(2,1)}), bf16[32,136,128]{2,1,0:T(8,128)(2,1)S(1)}, u32[]{:S(2)}, u32[]{:S(2)}) async-start(bf16[32,136,128]{2,1,0:T(8,128)(2,1)} %get-tuple-element.15), calls=%async_computation | async-start | bytes 2228224 | tf_op jit(solution)/shard_map/all_to_all | solution.py:267
  58.5 8.3 %collective-permute-start.1 = (bf16[32,32,128]{2,1,0:T(8,128)(2,1)S(1)}, bf16[32,32,128]{2,1,0:T(8,128)(2,1)S(1)}, u32[]{:S(2)}, u32[]{:S(2)}) collective-permute-start(bf16[32,32,128]{2,1,0:T(8,128)(2,1)S(1)} %foreign.1), channel_id=1, source_target_pairs={{0,16},{16,0},{1,17},{17,1},{2,18},{18,2},{3,19},{19,3},{4,20},{20... | collective-permute-start | bytes 786440 | tf_op jit(solution)/shard_map/ppermute | solution.py:279

commit v6 on v5

--- a/solution.py
+++ b/solution.py
@@ -61,7 +61,7 @@
         spread = jnp.dot(weights, ones_where(row == 4 * g + lane128 // 32), preferred_element_type=jnp.float32)
         a_ref[0, g * 16:(g + 1) * 16, :] = (out * spread).astype(jnp.bfloat16)
     a_plain = jnp.dot(weights, ones_where(lane128 == (row % 4) * 8 + row // 4), preferred_element_type=jnp.float32)
-    a_ref[0, 128:136, :] = (a_plain[:8] + pltpu.roll(a_plain[8:], 64, 1)).astype(jnp.bfloat16)
+    a_ref[0, 128:144, :] = a_plain.astype(jnp.bfloat16)
     for k in range(1, 4):
         a_ref[k] = a_ref[0]
     copies = [pltpu.make_async_copy(a_ref, copies_ref.at[pl.ds(4 * k, 4)], sems.at[8 + k]) for k in range(8)]
@@ -82,7 +82,7 @@
     for g in range(8):
         b_ref[g * 16:(g + 1) * 16, :] = (tiles[g * 16:(g + 1) * 16, :] * b_weights).astype(jnp.bfloat16)
     b_plain = jnp.where(iota((16, 128), 1) < 32, b_weights, 0.0)
-    b_ref[128:136, :] = (b_plain[:8] + pltpu.roll(b_plain[8:], 64, 1)).astype(jnp.bfloat16)
+    b_ref[128:144, :] = b_plain.astype(jnp.bfloat16)
     last.wait()
     wf[...] = ow_ref[...].astype(jnp.float32)
     for p in range(4):
@@ -94,7 +94,7 @@
 
 def project(x, mask, present, gain, bias, weight, proj_bias, out_bias, out_weight):
     vmem = pl.BlockSpec(memory_space=pltpu.VMEM)
-    out = [jax.ShapeDtypeStruct((32, 136, 128), jnp.bfloat16), jax.ShapeDtypeStruct((136, 128), jnp.bfloat16),
+    out = [jax.ShapeDtypeStruct((32, 144, 128), jnp.bfloat16), jax.ShapeDtypeStruct((144, 128), jnp.bfloat16),
            jax.ShapeDtypeStruct((128, 128), jnp.float32), jax.ShapeDtypeStruct((512, 256), jnp.bfloat16)]
     given = (x, mask, present[None], gain[None], bias[None], weight.T, proj_bias[None], out_bias[None], out_weight)
     return pl.pallas_call(
@@ -104,7 +104,7 @@
         out_specs=[pl.BlockSpec(memory_space=pl.ANY), vmem, vmem, vmem],
         scratch_shapes=[pltpu.VMEM(g.shape, g.dtype) for g in given] + [
             pltpu.VMEM((512, 128), jnp.float32), pltpu.VMEM((128, 128), jnp.float32),
-            pltpu.VMEM((4, 136, 128), jnp.bfloat16), pltpu.VMEM((1024, 128), jnp.float32), pltpu.SemaphoreType.DMA((17,))],
+            pltpu.VMEM((4, 144, 128), jnp.bfloat16), pltpu.VMEM((1024, 128), jnp.float32), pltpu.SemaphoreType.DMA((17,))],
         compiler_params=pltpu.CompilerParams(vmem_limit_bytes=56 * 1024 * 1024),
         cost_estimate=pl.CostEstimate(flops=4 * 10**7, bytes_accessed=2**19, transcendentals=0),
         name="project",
@@ -124,7 +124,7 @@
     return (y & 3) * 4 + (xh & 1) * 2 + (rank & 1)
 
 
-def columns_kernel(line_ref, b_ref, tile_ref, w_ref, o_ref, wb_ref, bias_ref, w4_ref, packed):
+def columns_kernel(line_ref, b_ref, tile_ref, w_ref, o_ref, wb_ref, bias_ref, w4_ref):
     for z in range(16):
         at = source(line_ref[0], jnp.int32(z))
         rows = pl.ds(pl.multiple_of(at * 16, 16), 16)
@@ -132,8 +132,7 @@
             v = b_ref[z, g * 16:(g + 1) * 16, :]
             o_ref[0, rows, g * 128:(g + 1) * 128] = v
             o_ref[1, rows, g * 128:(g + 1) * 128] = pltpu.roll(v.astype(jnp.float32), 64, 1).astype(jnp.bfloat16)
-        packed[pl.ds(pl.multiple_of(at * 8, 8), 8), :] = b_ref[z, 128:136, :].astype(jnp.float32)
-    wb_ref[...] = packed[...].astype(jnp.bfloat16)
+        wb_ref[rows, :] = b_ref[z, 128:144, :]
     bias_ref[...] = tile_ref[...]
     w4_ref[...] = w_ref[...]
 
@@ -142,11 +141,10 @@
     vmem = pl.BlockSpec(memory_space=pltpu.VMEM)
     return pl.pallas_call(
         columns_kernel,
-        out_shape=[jax.ShapeDtypeStruct((2, 256, 1024), jnp.bfloat16), jax.ShapeDtypeStruct((128, 128), jnp.bfloat16),
+        out_shape=[jax.ShapeDtypeStruct((2, 256, 1024), jnp.bfloat16), jax.ShapeDtypeStruct((256, 128), jnp.bfloat16),
                    jax.ShapeDtypeStruct((128, 128), jnp.float32), jax.ShapeDtypeStruct((512, 256), jnp.bfloat16)],
         in_specs=[pl.BlockSpec(memory_space=pltpu.SMEM), vmem, vmem, vmem],
         out_specs=[vmem] * 4,
-        scratch_shapes=[pltpu.VMEM((128, 128), jnp.float32)],
         compiler_params=pltpu.CompilerParams(vmem_limit_bytes=16 * 1024 * 1024),
         cost_estimate=pl.CostEstimate(flops=3*10**10, bytes_accessed=2**21, transcendentals=0),
         name="columns",
@@ -161,9 +159,8 @@
             i = 4 * g + k
             row = (i % 2) * 512 + (i // 2) * 32
             at[row:row + 32, :] = t[k * 32:(k + 1) * 32, :]
-    wa = a_ref[block, :, 128:136, :].astype(jnp.float32).reshape(128, 128).astype(jnp.bfloat16)
+    wa = a_ref[block, :, 128:144, :].reshape(256, 128)
     count = lax.dot_general(wa, wb_ref[...], (((0,), (0,)), ((), ())), preferred_element_type=jnp.float32)
-    count = jnp.where(lane[:32] < 32, count[0:32] + pltpu.roll(count[64:96], 64, 1), 0.0)
     spread = count[0:8]
     for k in range(1, 4):
         spread += pltpu.roll(count[k * 8:(k + 1) * 8], 32 * (0, 2, 1, 3)[k], 1)
@@ -264,7 +261,7 @@
     turn = [((z * 2 + xl) * 16 + q, (at * 2 + xl) * 16 + z) for z, row in enumerate(places()) for xl in range(2)
             for at, q in enumerate(row)]
     b = lax.ppermute(b, RES + SEQ, turn)
-    a_all = lax.all_to_all(a, ("xl",) + SEQ, 0, 0, tiled=True).reshape(2, 16, 136, 128)
+    a_all = lax.all_to_all(a, ("xl",) + SEQ, 0, 0, tiled=True).reshape(2, 16, 144, 128)
     b_all = lax.all_gather(b, "z")
     line = sum(lax.axis_index(n) * k for n, k in zip(SEQ, (4, 2, 1))).astype(jnp.int32).reshape(1)
     b_all, wb, bias2, w4 = columns(line, b_all, bias2, w4)

time: 67.9 us -> 68.1 us (level)
  the two profiles are of different devices: /device:TPU:12 before, /device:TPU:16 now
where the time goes in v6:
time: 68.1 us; the launch traced here: 67.9 us
  blocking collectives  32.7 us (48%)
  starting transfers between devices  23.5 us (35%)
  Pallas kernels  9.07 us (13%)
  waiting for transfers between devices  2.55 us (4%)
    all_gather x1, blocking collectives, local(): b_all = lax.all_gather(b, 'z')  32.7 us
    ppermute x1, starting transfers between devices, local(): b = lax.ppermute(b, RES + SEQ, turn)  12.1 us
    all_to_all x1, starting transfers between devices, local(): lax.all_to_all(a, ('xl',) + SEQ, 0, 0, tiled=True).reshape(2, 16, 144, 128)  8.28 us
    pallas_call x3, Pallas kernels, call(): pl.pallas_call(kernel, out_shape=jax.ShapeDtypeStruct(shape, dtype), in_s...  5.32 us
    pallas_call x1, Pallas kernels, project(): pl.pallas_call(project_kernel, out_shape=out, in_specs=[pl.BlockSpec(memo...  3.5 us
    ppermute x1, starting transfers between devices, local(): taken = lax.ppermute(sent, 'xl', shift(2, 1))  3.12 us
    ppermute x1, waiting for transfers between devices, local(): taken = lax.ppermute(sent, 'xl', shift(2, 1))  2.54 us
  transfers between devices with their start and end apart: 3, of which 1 were waited for; matrix products, arithmetic and copies ran while one was open for 0% of the time, Pallas kernels for 4%

profile of v6, /device:TPU:16, one launch (start us, length us, event | category | flops | bytes accessed | tf_op | source)
XLA Modules:
  0.0 67.9 jit_solution(13635532007687484938)
XLA Ops:
  0.0 3.5 %project.1 = (bf16[32,144,128]{2,1,0:T(8,128)(2,1)}, bf16[144,128]{1,0:T(8,128)(2,1)}, f32[128,128]{1,0:T(8,128)}, bf16[512,256]{1,0:T(8,128)(2,1)}) custom-call(bf16[16,32,256]{2,1,0:T(8,128)(2,1)} %refs_0_.1, s32[16,32]{1,0:T(8,128)} %refs_1_.1, s32[1,32]{1,0:T(1,128)} %bitcast.16, f32[1,256]{1,0:T(1,128)} %bitcast.14, f32[1,256]{1,0:T(1,128)} %bitcast.15, ...), custom_call_target="tpu_custom_call" | custom-call | flops 40000000 | bytes 524288 | tf_op jit(solution)/shard_map/project/pallas_call | solution.py:100
  3.5 12.1 %collective-permute-start = (bf16[144,128]{1,0:T(8,128)(2,1)}, bf16[144,128]{1,0:T(8,128)(2,1)S(1)}, u32[]{:S(2)}, u32[]{:S(2)}) collective-permute-start(bf16[144,128]{1,0:T(8,128)(2,1)} %get-tuple-element.16), channel_id=1, source_target_pairs={{10,0},{11,32},{7,64},{15,96},{9,128},{3,160},{5,192},{13,224},{1,... | collective-permute-start | bytes 110600 | tf_op jit(solution)/shard_map/ppermute | solution.py:263
  15.6 0.0 copy-start
  15.6 0.0 copy-start.1
  15.6 8.3 %all-to-all-start = ((bf16[32,144,128]{2,1,0:T(8,128)(2,1)}), bf16[32,144,128]{2,1,0:T(8,128)(2,1)S(1)}, u32[]{:S(2)}, u32[]{:S(2)}) async-start(bf16[32,144,128]{2,1,0:T(8,128)(2,1)} %get-tuple-element.15), calls=%async_computation | async-start | bytes 2359296 | tf_op jit(solution)/shard_map/all_to_all | solution.py:264
  23.9 0.0 collective-permute-done
  23.9 32.7 %all-gather = bf16[2304,128]{1,0:T(8,128)(2,1)S(1)} all-gather(bf16[144,128]{1,0:T(8,128)(2,1)S(1)} %collective-permute-done), channel_id=2, replica_groups=mesh['z'=16,'xl'=2,'y'=4,'xh'=2,'core'=2] {'z'}, dimensions={0}, use_global_device_ids=true | all-gather | bytes 626688 | tf_op jit(solution)/shard_map/all_gather | solution.py:265
  56.6 0.0 copy-done
  56.6 0.0 copy-done.1
  56.6 0.3 columns.1
  56.8 0.0 all-to-all-done
  56.9 1.9 %foreign.1 = bf16[32,32,128]{2,1,0:T(8,128)(2,1)S(1)} custom-call(s32[1]{0:T(128)} %bitcast.xl_ref, bf16[2,16,144,128]{3,2,1,0:T(8,128)(2,1)S(1)} %bitcast.10, bf16[2,256,1024]{2,1,0:T(8,128)(2,1)S(1)} %get-tuple-element.21.b_ref, bf16[256,128]{1,0:T(8,128)(2,1)S(1)} %get-tuple-element.22.wb_ref, bf16[512,256]{1,0:T(8,128)(2,1)S(1)} %get-tuple-element.23.w_ref, ...), custom_call_target="tpu_custom_call" | custom-call | flops 1000000000 | bytes 2097152 | tf_op jit(solution)/shard_map/foreign/pallas_call | solution.py:229
  58.7 3.1 %collective-permute-start.1 = (bf16[32,32,128]{2,1,0:T(8,128)(2,1)S(1)}, bf16[32,32,128]{2,1,0:T(8,128)(2,1)S(1)}, u32[]{:S(2)}, u32[]{:S(2)}) collective-permute-start(bf16[32,32,128]{2,1,0:T(8,128)(2,1)S(1)} %foreign.1), channel_id=1, source_target_pairs={{0,16},{16,0},{1,17},{17,1},{2,18},{18,2},{3,19},{19,3},{4,20},{20... | collective-permute-start | bytes 786440 | tf_op jit(solution)/shard_map/ppermute | solution.py:276
  61.9 2.6 %own.1.given_ref = f32[32,64,128]{2,1,0:T(8,128)} custom-call(s32[1]{0:T(128)} %bitcast.xl_ref, bf16[2,16,144,128]{3,2,1,0:T(8,128)(2,1)S(1)} %bitcast.11, bf16[2,256,1024]{2,1,0:T(8,128)(2,1)S(1)} %get-tuple-element.21.b_ref, bf16[256,128]{1,0:T(8,128)(2,1)S(1)} %get-tuple-element.22.wb_ref, bf16[512,256]{1,0:T(8,128)(2,1)S(1)} %get-tuple-element.23.w_ref, ...), custom_call_target="tpu_custom_call" | custom-call | flops 1000000000 | bytes 2097152 | tf_op jit(solution)/shard_map/own/pallas_call | solution.py:229
  64.5 2.5 %collective-permute-done.1.t_ref = bf16[32,32,128]{2,1,0:T(8,128)(2,1)S(1)} collective-permute-done((bf16[32,32,128]{2,1,0:T(8,128)(2,1)S(1)}, bf16[32,32,128]{2,1,0:T(8,128)(2,1)S(1)}, u32[]{:S(2)}, u32[]{:S(2)}) %collective-permute-start.1) | collective-permute-done | bytes 262176 | tf_op jit(solution)/shard_map/ppermute | solution.py:276
  67.0 0.9 %join.1 = f32[32,64,128]{2,1,0:T(8,128)} custom-call(s32[1]{0:T(128)} %bitcast.xl_ref, bf16[32,32,128]{2,1,0:T(8,128)(2,1)S(1)} %collective-permute-done.1.t_ref, f32[32,64,128]{2,1,0:T(8,128)} %own.1.given_ref), custom_call_target="tpu_custom_call", output_to_operand_aliasing={{}: (2, {})} | custom-call | flops 1000000 | bytes 2097152 | tf_op jit(solution)/shard_map/join/pallas_call | solution.py:229
Async XLA Ops:
  3.5 20.4 %collective-permute-start = (bf16[144,128]{1,0:T(8,128)(2,1)}, bf16[144,128]{1,0:T(8,128)(2,1)S(1)}, u32[]{:S(2)}, u32[]{:S(2)}) collective-permute-start(bf16[144,128]{1,0:T(8,128)(2,1)} %get-tuple-element.16), channel_id=1, source_target_pairs={{10,0},{11,32},{7,64},{15,96},{9,128},{3,160},{5,192},{13,224},{1,... | collective-permute-start | bytes 110600 | tf_op jit(solution)/shard_map/ppermute | solution.py:263
  15.6 41.0 %copy-start = (bf16[512,256]{1,0:T(8,128)(2,1)S(1)}, bf16[512,256]{1,0:T(8,128)(2,1)}, u32[]{:S(2)}) copy-start(bf16[512,256]{1,0:T(8,128)(2,1)} %get-tuple-element.18.w_ref) | copy-start | bytes 786436
  15.6 41.0 %copy-start.1 = (f32[128,128]{1,0:T(8,128)S(1)}, f32[128,128]{1,0:T(8,128)}, u32[]{:S(2)}) copy-start(f32[128,128]{1,0:T(8,128)} %get-tuple-element.17.tile_ref) | copy-start | bytes 196612
  15.6 41.2 %all-to-all-start = ((bf16[32,144,128]{2,1,0:T(8,128)(2,1)}), bf16[32,144,128]{2,1,0:T(8,128)(2,1)S(1)}, u32[]{:S(2)}, u32[]{:S(2)}) async-start(bf16[32,144,128]{2,1,0:T(8,128)(2,1)} %get-tuple-element.15), calls=%async_computation | async-start | bytes 2359296 | tf_op jit(solution)/shard_map/all_to_all | solution.py:264
  58.7 8.3 %collective-permute-start.1 = (bf16[32,32,128]{2,1,0:T(8,128)(2,1)S(1)}, bf16[32,32,128]{2,1,0:T(8,128)(2,1)S(1)}, u32[]{:S(2)}, u32[]{:S(2)}) collective-permute-start(bf16[32,32,128]{2,1,0:T(8,128)(2,1)S(1)} %foreign.1), channel_id=1, source_target_pairs={{0,16},{16,0},{1,17},{17,1},{2,18},{18,2},{3,19},{19,3},{4,20},{20... | collective-permute-start | bytes 786440 | tf_op jit(solution)/shard_map/ppermute | solution.py:276

commit v7 on v6

--- a/solution.py
+++ b/solution.py
@@ -19,7 +19,10 @@
 
 
 def project_kernel(*refs):
-    sources, (copies_ref, b_ref, tile_ref, w4_ref), held, (pa, tiles, a_ref, wf, sems) = refs[:9], refs[9:13], refs[13:22], refs[22:]
+    sources, (copies_ref, *results), held, (pa, tiles, a_ref, wf, b_ref, tile_ref, w4_ref, sems) = (
+        refs[:9], refs[9:13], refs[13:22], refs[22:])
+    leave = [pltpu.make_async_copy(src, dst, sems.at[17 + k])
+             for k, (src, dst) in enumerate(zip((b_ref, tile_ref, w4_ref), results))]
     small = [pltpu.make_async_copy(src, dst, sems.at[k]) for k, (src, dst) in enumerate(zip(sources[1:8], held[1:8]))]
     last = pltpu.make_async_copy(sources[8], held[8], sems.at[16])
     large = pltpu.make_async_copy(sources[0], held[0], sems.at[7])
@@ -46,6 +49,7 @@
     a_bias = jnp.dot(jnp.broadcast_to(pb_ref[...], (8, 64)), four.astype(jnp.float32),
                      precision=lax.Precision.HIGHEST, preferred_element_type=jnp.float32)
     tile_ref[...] = jnp.broadcast_to(ob_ref[...], (128, 128)).T
+    leave[1].start()
 
     value = x_ref[...].reshape(512, 256).astype(jnp.float32)
     mean = jnp.mean(value, axis=-1, keepdims=True)
@@ -83,17 +87,18 @@
         b_ref[g * 16:(g + 1) * 16, :] = (tiles[g * 16:(g + 1) * 16, :] * b_weights).astype(jnp.bfloat16)
     b_plain = jnp.where(iota((16, 128), 1) < 32, b_weights, 0.0)
     b_ref[128:144, :] = b_plain.astype(jnp.bfloat16)
+    leave[0].start()
     last.wait()
     wf[...] = ow_ref[...].astype(jnp.float32)
     for p in range(4):
         rows = jnp.concatenate([wf[pl.ds(4 * g + p, 32, stride=32), :] for g in range(8)], axis=0)
         w4_ref[p * 128:(p + 1) * 128, :] = rows.T.astype(jnp.bfloat16)
-    for copy in copies:
+    leave[2].start()
+    for copy in copies + leave:
         copy.wait()
 
 
 def project(x, mask, present, gain, bias, weight, proj_bias, out_bias, out_weight):
-    vmem = pl.BlockSpec(memory_space=pltpu.VMEM)
     out = [jax.ShapeDtypeStruct((32, 144, 128), jnp.bfloat16), jax.ShapeDtypeStruct((144, 128), jnp.bfloat16),
            jax.ShapeDtypeStruct((128, 128), jnp.float32), jax.ShapeDtypeStruct((512, 256), jnp.bfloat16)]
     given = (x, mask, present[None], gain[None], bias[None], weight.T, proj_bias[None], out_bias[None], out_weight)
@@ -101,10 +106,11 @@
         project_kernel,
         out_shape=out,
         in_specs=[pl.BlockSpec(memory_space=pl.ANY)] * 9,
-        out_specs=[pl.BlockSpec(memory_space=pl.ANY), vmem, vmem, vmem],
+        out_specs=[pl.BlockSpec(memory_space=pl.ANY)] * 4,
         scratch_shapes=[pltpu.VMEM(g.shape, g.dtype) for g in given] + [
             pltpu.VMEM((512, 128), jnp.float32), pltpu.VMEM((128, 128), jnp.float32),
-            pltpu.VMEM((4, 144, 128), jnp.bfloat16), pltpu.VMEM((1024, 128), jnp.float32), pltpu.SemaphoreType.DMA((17,))],
+            pltpu.VMEM((4, 144, 128), jnp.bfloat16), pltpu.VMEM((1024, 128), jnp.float32)] + [
+            pltpu.VMEM(o.shape, o.dtype) for o in out[1:]] + [pltpu.SemaphoreType.DMA((20,))],
         compiler_params=pltpu.CompilerParams(vmem_limit_bytes=56 * 1024 * 1024),
         cost_estimate=pl.CostEstimate(flops=4 * 10**7, bytes_accessed=2**19, transcendentals=0),
         name="project",

time: 68.1 us -> 67.6 us (level)
  no operation moved by 1% of the time
where the time goes in v7:
time: 67.6 us; the launch traced here: 67.3 us
  blocking collectives  32.7 us (48%)
  starting transfers between devices  23.5 us (35%)
  Pallas kernels  8.51 us (13%)
  waiting for transfers between devices  2.54 us (4%)
    all_gather x1, blocking collectives, local(): b_all = lax.all_gather(b, 'z')  32.7 us
    ppermute x1, starting transfers between devices, local(): b = lax.ppermute(b, RES + SEQ, turn)  12.1 us
    all_to_all x1, starting transfers between devices, local(): lax.all_to_all(a, ('xl',) + SEQ, 0, 0, tiled=True).reshape(2, 16, 144, 128)  8.29 us
    pallas_call x3, Pallas kernels, call(): pl.pallas_call(kernel, out_shape=jax.ShapeDtypeStruct(shape, dtype), in_s...  5.32 us
    ppermute x1, starting transfers between devices, local(): taken = lax.ppermute(sent, 'xl', shift(2, 1))  3.12 us
    pallas_call x1, Pallas kernels, project(): pl.pallas_call(project_kernel, out_shape=out, in_specs=[pl.BlockSpec(memo...  2.94 us
    ppermute x1, waiting for transfers between devices, local(): taken = lax.ppermute(sent, 'xl', shift(2, 1))  2.54 us
  transfers between devices with their start and end apart: 3, of which 1 were waited for; matrix products, arithmetic and copies ran while one was open for 0% of the time, Pallas kernels for 4%

profile of v7, /device:TPU:16, one launch (start us, length us, event | category | flops | bytes accessed | tf_op | source)
XLA Modules:
  0.0 67.3 jit_solution(3938463967120495388)
XLA Ops:
  0.0 2.9 %project.1 = (bf16[32,144,128]{2,1,0:T(8,128)(2,1)}, bf16[144,128]{1,0:T(8,128)(2,1)}, f32[128,128]{1,0:T(8,128)}, bf16[512,256]{1,0:T(8,128)(2,1)}) custom-call(bf16[16,32,256]{2,1,0:T(8,128)(2,1)} %refs_0_.1, s32[16,32]{1,0:T(8,128)} %refs_1_.1, s32[1,32]{1,0:T(1,128)} %bitcast.16, f32[1,256]{1,0:T(1,128)} %bitcast.14, f32[1,256]{1,0:T(1,128)} %bitcast.15, ...), custom_call_target="tpu_custom_call" | custom-call | flops 40000000 | bytes 524288 | tf_op jit(solution)/shard_map/project/pallas_call | solution.py:105
  2.9 12.1 %collective-permute-start = (bf16[144,128]{1,0:T(8,128)(2,1)}, bf16[144,128]{1,0:T(8,128)(2,1)S(1)}, u32[]{:S(2)}, u32[]{:S(2)}) collective-permute-start(bf16[144,128]{1,0:T(8,128)(2,1)} %get-tuple-element.16), channel_id=1, source_target_pairs={{10,0},{11,32},{7,64},{15,96},{9,128},{3,160},{5,192},{13,224},{1,... | collective-permute-start | bytes 110600 | tf_op jit(solution)/shard_map/ppermute | solution.py:269
  15.0 0.0 copy-start
  15.0 0.0 copy-start.1
  15.0 8.3 %all-to-all-start = ((bf16[32,144,128]{2,1,0:T(8,128)(2,1)}), bf16[32,144,128]{2,1,0:T(8,128)(2,1)S(1)}, u32[]{:S(2)}, u32[]{:S(2)}) async-start(bf16[32,144,128]{2,1,0:T(8,128)(2,1)} %get-tuple-element.15), calls=%async_computation | async-start | bytes 2359296 | tf_op jit(solution)/shard_map/all_to_all | solution.py:270
  23.3 0.0 collective-permute-done
  23.4 32.7 %all-gather = bf16[2304,128]{1,0:T(8,128)(2,1)S(1)} all-gather(bf16[144,128]{1,0:T(8,128)(2,1)S(1)} %collective-permute-done), channel_id=2, replica_groups=mesh['z'=16,'xl'=2,'y'=4,'xh'=2,'core'=2] {'z'}, dimensions={0}, use_global_device_ids=true | all-gather | bytes 626688 | tf_op jit(solution)/shard_map/all_gather | solution.py:271
  56.0 0.0 copy-done
  56.0 0.0 copy-done.1
  56.0 0.3 columns.1
  56.3 0.0 all-to-all-done
  56.3 1.9 %foreign.1 = bf16[32,32,128]{2,1,0:T(8,128)(2,1)S(1)} custom-call(s32[1]{0:T(128)} %bitcast.xl_ref, bf16[2,16,144,128]{3,2,1,0:T(8,128)(2,1)S(1)} %bitcast.10, bf16[2,256,1024]{2,1,0:T(8,128)(2,1)S(1)} %get-tuple-element.21.b_ref, bf16[256,128]{1,0:T(8,128)(2,1)S(1)} %get-tuple-element.22.wb_ref, bf16[512,256]{1,0:T(8,128)(2,1)S(1)} %get-tuple-element.23.w_ref, ...), custom_call_target="tpu_custom_call" | custom-call | flops 1000000000 | bytes 2097152 | tf_op jit(solution)/shard_map/foreign/pallas_call | solution.py:235
  58.2 3.1 %collective-permute-start.1 = (bf16[32,32,128]{2,1,0:T(8,128)(2,1)S(1)}, bf16[32,32,128]{2,1,0:T(8,128)(2,1)S(1)}, u32[]{:S(2)}, u32[]{:S(2)}) collective-permute-start(bf16[32,32,128]{2,1,0:T(8,128)(2,1)S(1)} %foreign.1), channel_id=1, source_target_pairs={{0,16},{16,0},{1,17},{17,1},{2,18},{18,2},{3,19},{19,3},{4,20},{20... | collective-permute-start | bytes 786440 | tf_op jit(solution)/shard_map/ppermute | solution.py:282
  61.3 2.6 %own.1.given_ref = f32[32,64,128]{2,1,0:T(8,128)} custom-call(s32[1]{0:T(128)} %bitcast.xl_ref, bf16[2,16,144,128]{3,2,1,0:T(8,128)(2,1)S(1)} %bitcast.11, bf16[2,256,1024]{2,1,0:T(8,128)(2,1)S(1)} %get-tuple-element.21.b_ref, bf16[256,128]{1,0:T(8,128)(2,1)S(1)} %get-tuple-element.22.wb_ref, bf16[512,256]{1,0:T(8,128)(2,1)S(1)} %get-tuple-element.23.w_ref, ...), custom_call_target="tpu_custom_call" | custom-call | flops 1000000000 | bytes 2097152 | tf_op jit(solution)/shard_map/own/pallas_call | solution.py:235
  63.9 2.5 %collective-permute-done.1.t_ref = bf16[32,32,128]{2,1,0:T(8,128)(2,1)S(1)} collective-permute-done((bf16[32,32,128]{2,1,0:T(8,128)(2,1)S(1)}, bf16[32,32,128]{2,1,0:T(8,128)(2,1)S(1)}, u32[]{:S(2)}, u32[]{:S(2)}) %collective-permute-start.1) | collective-permute-done | bytes 262176 | tf_op jit(solution)/shard_map/ppermute | solution.py:282
  66.4 0.9 %join.1 = f32[32,64,128]{2,1,0:T(8,128)} custom-call(s32[1]{0:T(128)} %bitcast.xl_ref, bf16[32,32,128]{2,1,0:T(8,128)(2,1)S(1)} %collective-permute-done.1.t_ref, f32[32,64,128]{2,1,0:T(8,128)} %own.1.given_ref), custom_call_target="tpu_custom_call", output_to_operand_aliasing={{}: (2, {})} | custom-call | flops 1000000 | bytes 2097152 | tf_op jit(solution)/shard_map/join/pallas_call | solution.py:235
Async XLA Ops:
  2.9 20.4 %collective-permute-start = (bf16[144,128]{1,0:T(8,128)(2,1)}, bf16[144,128]{1,0:T(8,128)(2,1)S(1)}, u32[]{:S(2)}, u32[]{:S(2)}) collective-permute-start(bf16[144,128]{1,0:T(8,128)(2,1)} %get-tuple-element.16), channel_id=1, source_target_pairs={{10,0},{11,32},{7,64},{15,96},{9,128},{3,160},{5,192},{13,224},{1,... | collective-permute-start | bytes 110600 | tf_op jit(solution)/shard_map/ppermute | solution.py:269
  15.0 41.0 %copy-start = (bf16[512,256]{1,0:T(8,128)(2,1)S(1)}, bf16[512,256]{1,0:T(8,128)(2,1)}, u32[]{:S(2)}) copy-start(bf16[512,256]{1,0:T(8,128)(2,1)} %get-tuple-element.18.w_ref) | copy-start | bytes 786436
  15.0 41.0 %copy-start.1 = (f32[128,128]{1,0:T(8,128)S(1)}, f32[128,128]{1,0:T(8,128)}, u32[]{:S(2)}) copy-start(f32[128,128]{1,0:T(8,128)} %get-tuple-element.17.tile_ref) | copy-start | bytes 196612
  15.0 41.2 %all-to-all-start = ((bf16[32,144,128]{2,1,0:T(8,128)(2,1)}), bf16[32,144,128]{2,1,0:T(8,128)(2,1)S(1)}, u32[]{:S(2)}, u32[]{:S(2)}) async-start(bf16[32,144,128]{2,1,0:T(8,128)(2,1)} %get-tuple-element.15), calls=%async_computation | async-start | bytes 2359296 | tf_op jit(solution)/shard_map/all_to_all | solution.py:270
  58.2 8.3 %collective-permute-start.1 = (bf16[32,32,128]{2,1,0:T(8,128)(2,1)S(1)}, bf16[32,32,128]{2,1,0:T(8,128)(2,1)S(1)}, u32[]{:S(2)}, u32[]{:S(2)}) collective-permute-start(bf16[32,32,128]{2,1,0:T(8,128)(2,1)S(1)} %foreign.1), channel_id=1, source_target_pairs={{0,16},{16,0},{1,17},{17,1},{2,18},{18,2},{3,19},{19,3},{4,20},{20... | collective-permute-start | bytes 786440 | tf_op jit(solution)/shard_map/ppermute | solution.py:282

commit v8 on v7

--- a/solution.py
+++ b/solution.py
@@ -72,6 +72,13 @@
     for copy in copies:
         copy.start()
 
+    last.wait()
+    wf[...] = ow_ref[...].astype(jnp.float32)
+    for p in range(4):
+        rows = jnp.concatenate([wf[pl.ds(4 * g + p, 32, stride=32), :] for g in range(8)], axis=0)
+        w4_ref[p * 128:(p + 1) * 128, :] = rows.T.astype(jnp.bfloat16)
+    leave[2].start()
+
     bt = lax.dot_general(wb, normed, (((1,), (1,)), ((), ())), preferred_element_type=jnp.float32)
     group = iota((8, 128), 1) // 32
     for t in range(4):
@@ -88,12 +95,6 @@
     b_plain = jnp.where(iota((16, 128), 1) < 32, b_weights, 0.0)
     b_ref[128:144, :] = b_plain.astype(jnp.bfloat16)
     leave[0].start()
-    last.wait()
-    wf[...] = ow_ref[...].astype(jnp.float32)
-    for p in range(4):
-        rows = jnp.concatenate([wf[pl.ds(4 * g + p, 32, stride=32), :] for g in range(8)], axis=0)
-        w4_ref[p * 128:(p + 1) * 128, :] = rows.T.astype(jnp.bfloat16)
-    leave[2].start()
     for copy in copies + leave:
         copy.wait()
 

time: 67.6 us -> 67.5 us (level)
  no operation moved by 1% of the time
where the time goes in v8:
time: 67.5 us; the launch traced here: 67.2 us
  blocking collectives  32.7 us (48%)
  starting transfers between devices  23.5 us (35%)
  Pallas kernels  8.43 us (12%)
  waiting for transfers between devices  2.54 us (4%)
    all_gather x1, blocking collectives, local(): b_all = lax.all_gather(b, 'z')  32.7 us
    ppermute x1, starting transfers between devices, local(): b = lax.ppermute(b, RES + SEQ, turn)  12.1 us
    all_to_all x1, starting transfers between devices, local(): lax.all_to_all(a, ('xl',) + SEQ, 0, 0, tiled=True).reshape(2, 16, 144, 128)  8.29 us
    pallas_call x3, Pallas kernels, call(): pl.pallas_call(kernel, out_shape=jax.ShapeDtypeStruct(shape, dtype), in_s...  5.32 us
    ppermute x1, starting transfers between devices, local(): taken = lax.ppermute(sent, 'xl', shift(2, 1))  3.13 us
    pallas_call x1, Pallas kernels, project(): pl.pallas_call(project_kernel, out_shape=out, in_specs=[pl.BlockSpec(memo...  2.86 us
    ppermute x1, waiting for transfers between devices, local(): taken = lax.ppermute(sent, 'xl', shift(2, 1))  2.54 us
  transfers between devices with their start and end apart: 3, of which 1 were waited for; matrix products, arithmetic and copies ran while one was open for 0% of the time, Pallas kernels for 4%

profile of v8, /device:TPU:16, one launch (start us, length us, event | category | flops | bytes accessed | tf_op | source)
XLA Modules:
  0.0 67.2 jit_solution(2889524939278763656)
XLA Ops:
  0.0 2.9 %project.1 = (bf16[32,144,128]{2,1,0:T(8,128)(2,1)}, bf16[144,128]{1,0:T(8,128)(2,1)}, f32[128,128]{1,0:T(8,128)}, bf16[512,256]{1,0:T(8,128)(2,1)}) custom-call(bf16[16,32,256]{2,1,0:T(8,128)(2,1)} %refs_0_.1, s32[16,32]{1,0:T(8,128)} %refs_1_.1, s32[1,32]{1,0:T(1,128)} %bitcast.16, f32[1,256]{1,0:T(1,128)} %bitcast.14, f32[1,256]{1,0:T(1,128)} %bitcast.15, ...), custom_call_target="tpu_custom_call" | custom-call | flops 40000000 | bytes 524288 | tf_op jit(solution)/shard_map/project/pallas_call | solution.py:106
  2.9 12.1 %collective-permute-start = (bf16[144,128]{1,0:T(8,128)(2,1)}, bf16[144,128]{1,0:T(8,128)(2,1)S(1)}, u32[]{:S(2)}, u32[]{:S(2)}) collective-permute-start(bf16[144,128]{1,0:T(8,128)(2,1)} %get-tuple-element.16), channel_id=1, source_target_pairs={{10,0},{11,32},{7,64},{15,96},{9,128},{3,160},{5,192},{13,224},{1,... | collective-permute-start | bytes 110600 | tf_op jit(solution)/shard_map/ppermute | solution.py:270
  14.9 0.0 copy-start
  14.9 0.0 copy-start.1
  15.0 8.3 %all-to-all-start = ((bf16[32,144,128]{2,1,0:T(8,128)(2,1)}), bf16[32,144,128]{2,1,0:T(8,128)(2,1)S(1)}, u32[]{:S(2)}, u32[]{:S(2)}) async-start(bf16[32,144,128]{2,1,0:T(8,128)(2,1)} %get-tuple-element.15), calls=%async_computation | async-start | bytes 2359296 | tf_op jit(solution)/shard_map/all_to_all | solution.py:271
  23.3 0.0 collective-permute-done
  23.3 32.7 %all-gather = bf16[2304,128]{1,0:T(8,128)(2,1)S(1)} all-gather(bf16[144,128]{1,0:T(8,128)(2,1)S(1)} %collective-permute-done), channel_id=2, replica_groups=mesh['z'=16,'xl'=2,'y'=4,'xh'=2,'core'=2] {'z'}, dimensions={0}, use_global_device_ids=true | all-gather | bytes 626688 | tf_op jit(solution)/shard_map/all_gather | solution.py:272
  55.9 0.0 copy-done
  55.9 0.0 copy-done.1
  55.9 0.3 columns.1
  56.2 0.0 all-to-all-done
  56.2 1.9 %foreign.1 = bf16[32,32,128]{2,1,0:T(8,128)(2,1)S(1)} custom-call(s32[1]{0:T(128)} %bitcast.xl_ref, bf16[2,16,144,128]{3,2,1,0:T(8,128)(2,1)S(1)} %bitcast.10, bf16[2,256,1024]{2,1,0:T(8,128)(2,1)S(1)} %get-tuple-element.21.b_ref, bf16[256,128]{1,0:T(8,128)(2,1)S(1)} %get-tuple-element.22.wb_ref, bf16[512,256]{1,0:T(8,128)(2,1)S(1)} %get-tuple-element.23.w_ref, ...), custom_call_target="tpu_custom_call" | custom-call | flops 1000000000 | bytes 2097152 | tf_op jit(solution)/shard_map/foreign/pallas_call | solution.py:236
  58.1 3.1 %collective-permute-start.1 = (bf16[32,32,128]{2,1,0:T(8,128)(2,1)S(1)}, bf16[32,32,128]{2,1,0:T(8,128)(2,1)S(1)}, u32[]{:S(2)}, u32[]{:S(2)}) collective-permute-start(bf16[32,32,128]{2,1,0:T(8,128)(2,1)S(1)} %foreign.1), channel_id=1, source_target_pairs={{0,16},{16,0},{1,17},{17,1},{2,18},{18,2},{3,19},{19,3},{4,20},{20... | collective-permute-start | bytes 786440 | tf_op jit(solution)/shard_map/ppermute | solution.py:283
  61.2 2.6 %own.1.given_ref = f32[32,64,128]{2,1,0:T(8,128)} custom-call(s32[1]{0:T(128)} %bitcast.xl_ref, bf16[2,16,144,128]{3,2,1,0:T(8,128)(2,1)S(1)} %bitcast.11, bf16[2,256,1024]{2,1,0:T(8,128)(2,1)S(1)} %get-tuple-element.21.b_ref, bf16[256,128]{1,0:T(8,128)(2,1)S(1)} %get-tuple-element.22.wb_ref, bf16[512,256]{1,0:T(8,128)(2,1)S(1)} %get-tuple-element.23.w_ref, ...), custom_call_target="tpu_custom_call" | custom-call | flops 1000000000 | bytes 2097152 | tf_op jit(solution)/shard_map/own/pallas_call | solution.py:236
  63.8 2.5 %collective-permute-done.1.t_ref = bf16[32,32,128]{2,1,0:T(8,128)(2,1)S(1)} collective-permute-done((bf16[32,32,128]{2,1,0:T(8,128)(2,1)S(1)}, bf16[32,32,128]{2,1,0:T(8,128)(2,1)S(1)}, u32[]{:S(2)}, u32[]{:S(2)}) %collective-permute-start.1) | collective-permute-done | bytes 262176 | tf_op jit(solution)/shard_map/ppermute | solution.py:283
  66.4 0.9 %join.1 = f32[32,64,128]{2,1,0:T(8,128)} custom-call(s32[1]{0:T(128)} %bitcast.xl_ref, bf16[32,32,128]{2,1,0:T(8,128)(2,1)S(1)} %collective-permute-done.1.t_ref, f32[32,64,128]{2,1,0:T(8,128)} %own.1.given_ref), custom_call_target="tpu_custom_call", output_to_operand_aliasing={{}: (2, {})} | custom-call | flops 1000000 | bytes 2097152 | tf_op jit(solution)/shard_map/join/pallas_call | solution.py:236
Async XLA Ops:
  2.9 20.4 %collective-permute-start = (bf16[144,128]{1,0:T(8,128)(2,1)}, bf16[144,128]{1,0:T(8,128)(2,1)S(1)}, u32[]{:S(2)}, u32[]{:S(2)}) collective-permute-start(bf16[144,128]{1,0:T(8,128)(2,1)} %get-tuple-element.16), channel_id=1, source_target_pairs={{10,0},{11,32},{7,64},{15,96},{9,128},{3,160},{5,192},{13,224},{1,... | collective-permute-start | bytes 110600 | tf_op jit(solution)/shard_map/ppermute | solution.py:270
  14.9 41.0 %copy-start = (bf16[512,256]{1,0:T(8,128)(2,1)S(1)}, bf16[512,256]{1,0:T(8,128)(2,1)}, u32[]{:S(2)}) copy-start(bf16[512,256]{1,0:T(8,128)(2,1)} %get-tuple-element.18.w_ref) | copy-start | bytes 786436
  14.9 41.0 %copy-start.1 = (f32[128,128]{1,0:T(8,128)S(1)}, f32[128,128]{1,0:T(8,128)}, u32[]{:S(2)}) copy-start(f32[128,128]{1,0:T(8,128)} %get-tuple-element.17.tile_ref) | copy-start | bytes 196612
  15.0 41.2 %all-to-all-start = ((bf16[32,144,128]{2,1,0:T(8,128)(2,1)}), bf16[32,144,128]{2,1,0:T(8,128)(2,1)S(1)}, u32[]{:S(2)}, u32[]{:S(2)}) async-start(bf16[32,144,128]{2,1,0:T(8,128)(2,1)} %get-tuple-element.15), calls=%async_computation | async-start | bytes 2359296 | tf_op jit(solution)/shard_map/all_to_all | solution.py:271
  58.1 8.3 %collective-permute-start.1 = (bf16[32,32,128]{2,1,0:T(8,128)(2,1)S(1)}, bf16[32,32,128]{2,1,0:T(8,128)(2,1)S(1)}, u32[]{:S(2)}, u32[]{:S(2)}) collective-permute-start(bf16[32,32,128]{2,1,0:T(8,128)(2,1)S(1)} %foreign.1), channel_id=1, source_target_pairs={{0,16},{16,0},{1,17},{17,1},{2,18},{18,2},{3,19},{19,3},{4,20},{20... | collective-permute-start | bytes 786440 | tf_op jit(solution)/shard_map/ppermute | solution.py:283
